TPU v7x, 128 devices: a whole 4x4x4 slice. The times are simulated.
128 devices in a mesh: grp: 2 (over x_hi), row: 32 (over y, z, x_lo), col: 2 (over core).
Axes of the slice: x: 4 (x_hi: 2, x_lo: 2; x = x_hi * 2 + x_lo), y: 4, z: 4, core: 2. Of those that a mesh axis runs over, the one named last changes fastest.
Arguments:
- order_field: float32 [4, 16, 1024, 1024], P('grp', None, 'row', 'col'), may hold values from 0 to 1
- grain_label: int32 [4, 1024, 1024], P('grp', 'row', 'col'), may hold values from 0 to 31
- phase_label: int32 [4, 1024, 1024], P('grp', 'row', 'col'), may hold values from 0 to 7
- grain_mobility: float32 [32], replicated, may hold values from 0.25 to 1
- stiff_index: int32 [8], replicated, may hold values from 0 to 3
- stiff_table: float32 [4, 2], replicated, may hold values from 0.5 to 2
- eigen_strain: float32 [16, 3], replicated, may hold values from -1.5 to 1.5
- macro_strain: float32 [3], replicated, may hold values from -2 to 2
Outputs:
- order_next: float32 [4, 16, 1024, 1024], P('grp', None, 'row', 'col')
- strain_field: float32 [4, 3, 1024, 1024], P('grp', None, 'row', 'col')
All inputs are finite; a program needn't handle non-finite values.
Results may differ from a plain program's by a relative error of at most 0.00014.
Values sent between devices are 32-bit elements; how exact they have to be, the bound alone decides.
A program may use at most 128 MiB of HBM per device.

v0:
```python
import math

import jax
import jax.numpy as jnp
from jax import lax
from jax.sharding import PartitionSpec as P

ITERS = 2


GAMMA_MIX = 1.5
KAPPA_GRAD = 1.0
STEP_TIME = 0.1
LAYER_COUPLE = 0.5
LAMBDA_REF = 1.25
SHEAR_REF = 1.25
BETA_REF = (LAMBDA_REF + SHEAR_REF) / (SHEAR_REF * (LAMBDA_REF + 2.0 * SHEAR_REF))
PRECISE = lax.Precision.HIGHEST


def with_halo(value, sides, width, wrap):
    for axis, dim in sides:
        size, length = (lax.axis_size(axis), value.shape[dim])
        up = [(i, (i + 1) % size) for i in range(size if wrap else size - 1)]
        down = [(j, i) for i, j in up]
        last = lax.slice_in_dim(value, length - width, length, axis=dim)
        initial = lax.slice_in_dim(value, 0, width, axis=dim)
        before = lax.ppermute(last, axis, up)
        after = lax.ppermute(initial, axis, down)
        value = jnp.concatenate([before, value, after], axis=dim)
    return value


def advance(fields, mobility, pad_fields, pad_mobility, below, above, driving_term):
    extent_rows = fields.shape[2]
    extent_cols = fields.shape[3]
    diffuse = jnp.zeros_like(fields)
    for offset_rows, offset_cols in ((0, 1), (2, 1), (1, 0), (1, 2)):
        beside = pad_fields[
            :, :, offset_rows : offset_rows + extent_rows, offset_cols : offset_cols + extent_cols
        ]
        mob_beside = pad_mobility[
            :,
            None,
            offset_rows : offset_rows + extent_rows,
            offset_cols : offset_cols + extent_cols,
        ]
        diffuse = diffuse + 0.5 * (mobility[:, None] + mob_beside) * (beside - fields)
    squares = fields * fields
    totals = jnp.sum(squares, axis=1, keepdims=True)
    bulk_term = squares * fields - fields + 2.0 * GAMMA_MIX * fields * (totals - squares)
    layered = LAYER_COUPLE * (below + above - 2.0 * fields)
    return fields + STEP_TIME * (
        KAPPA_GRAD * diffuse + mobility[:, None] * (layered - bulk_term + driving_term)
    )


def directions(freq_rows, freq_cols, extent_rows, extent_cols):
    signed_rows = jnp.where(
        freq_rows >= extent_rows // 2, freq_rows - extent_rows, freq_rows
    ).astype(jnp.float32)
    signed_cols = jnp.where(
        freq_cols >= extent_cols // 2, freq_cols - extent_cols, freq_cols
    ).astype(jnp.float32)
    keeper = ((freq_rows != extent_rows // 2) & (freq_cols != extent_cols // 2)).astype(jnp.float32)
    radius = signed_rows * signed_rows + signed_cols * signed_cols
    inverse = keeper * lax.rsqrt(jnp.where(radius > 0, radius, 1.0))
    return (signed_rows * inverse, signed_cols * inverse)


def green(stress_rr, stress_cc, stress_rc, unit_row, unit_col):
    push_row = stress_rr * unit_row + stress_rc * unit_col
    push_col = stress_rc * unit_row + stress_cc * unit_col
    normal_part = unit_row * push_row + unit_col * push_col
    out_rr = unit_row * push_row / SHEAR_REF - BETA_REF * unit_row * unit_row * normal_part
    out_cc = unit_col * push_col / SHEAR_REF - BETA_REF * unit_col * unit_col * normal_part
    out_rc = (
        0.5 * (unit_row * push_col + unit_col * push_row) / SHEAR_REF
        - BETA_REF * unit_row * unit_col * normal_part
    )
    return (out_rr, out_cc, out_rc)


def stress_of(strain, eigen_field, lambda_cell, shear_cell):
    elastic = strain - eigen_field
    along_rr = (lambda_cell + 2.0 * shear_cell) * elastic[:, 0] + lambda_cell * elastic[:, 1]
    along_cc = lambda_cell * elastic[:, 0] + (lambda_cell + 2.0 * shear_cell) * elastic[:, 1]
    along_rc = 2.0 * shear_cell * elastic[:, 2]
    return jnp.stack([along_rr, along_cc, along_rc], axis=1)


def driving(stress, fields, eigen_strain):
    weighted = jnp.stack([stress[:, 0], stress[:, 1], 2.0 * stress[:, 2]], axis=1)
    project = jnp.einsum("lcxy,ic->lixy", weighted, eigen_strain, precision=PRECISE)
    return 2.0 * fields * project


def table_lookup(labels, values_table, entries):
    values = jnp.arange(entries, dtype=jnp.int32).reshape((entries,) + (1,) * labels.ndim)
    matched = labels[None] == values
    return jnp.sum(
        jnp.where(matched, values_table.reshape((entries,) + (1,) * labels.ndim), 0.0), axis=0
    )


def twiddle(first_ids, second_ids, length):
    product = first_ids[:, None] * second_ids[None, :] % length
    angle = product.astype(jnp.float32) * (2.0 * math.pi / length)
    return (jnp.cos(angle), jnp.sin(angle))


def split_length(length):
    inner = 1
    factor = 2
    while factor * factor <= length:
        if length % factor == 0:
            inner = factor
        factor = factor + 1
    return (inner, length // inner)


def row_tables(length):
    inner, outer = split_length(length)
    outer_ids = jnp.arange(outer, dtype=jnp.int32)
    inner_ids = jnp.arange(inner, dtype=jnp.int32)
    first_cos, first_sin = twiddle(outer_ids, outer_ids, outer)
    mid_cos, mid_sin = twiddle(outer_ids, inner_ids, length)
    last_cos, last_sin = twiddle(inner_ids, inner_ids, inner)
    return (inner, outer, first_cos, first_sin, mid_cos, mid_sin, last_cos, last_sin)


def row_transform(real_part, imag_part, tables, sign):
    inner, outer, first_cos, first_sin, mid_cos, mid_sin, last_cos, last_sin = tables
    lead = real_part.shape[:-1]
    real_part = real_part.reshape(lead + (outer, inner))
    imag_part = imag_part.reshape(lead + (outer, inner))
    segment_real = jnp.einsum(
        "...ap,ak->...kp", real_part, first_cos, precision=PRECISE
    ) - sign * jnp.einsum("...ap,ak->...kp", imag_part, first_sin, precision=PRECISE)
    segment_imag = jnp.einsum(
        "...ap,ak->...kp", imag_part, first_cos, precision=PRECISE
    ) + sign * jnp.einsum("...ap,ak->...kp", real_part, first_sin, precision=PRECISE)
    turned_real = segment_real * mid_cos - sign * segment_imag * mid_sin
    turned_imag = segment_imag * mid_cos + sign * segment_real * mid_sin
    final_real = jnp.einsum(
        "...kp,pb->...bk", turned_real, last_cos, precision=PRECISE
    ) - sign * jnp.einsum("...kp,pb->...bk", turned_imag, last_sin, precision=PRECISE)
    final_imag = jnp.einsum(
        "...kp,pb->...bk", turned_imag, last_cos, precision=PRECISE
    ) + sign * jnp.einsum("...kp,pb->...bk", turned_real, last_sin, precision=PRECISE)
    return (
        final_real.reshape(lead + (inner * outer,)),
        final_imag.reshape(lead + (inner * outer,)),
    )


def body(
    order_field,
    grain_label,
    phase_label,
    grain_mobility,
    stiff_index,
    stiff_table,
    eigen_strain,
    macro_strain,
):
    layer_count = order_field.shape[0]
    tile_rows = order_field.shape[2]
    tile_cols = order_field.shape[3]
    row_parts = lax.axis_size("row")
    col_parts = lax.axis_size("col")
    row_place = lax.axis_index("row")
    col_place = lax.axis_index("col")
    rows_total = tile_rows * row_parts
    cols_total = tile_cols * col_parts
    batch_size = layer_count * 3
    mobility = table_lookup(grain_label, grain_mobility, grain_mobility.shape[0])
    lambda_phase = table_lookup(stiff_index, stiff_table[:, 0], stiff_table.shape[0])
    shear_phase = table_lookup(stiff_index, stiff_table[:, 1], stiff_table.shape[0])
    lambda_cell = table_lookup(phase_label, lambda_phase, stiff_index.shape[0])
    shear_cell = table_lookup(phase_label, shear_phase, stiff_index.shape[0])

    def step_fields(fields, driving_term):
        stacked = jnp.concatenate([fields, mobility[:, None]], axis=1)
        padded = with_halo(stacked, (("row", 2), ("col", 3)), 1, True)
        layered = with_halo(fields, (("grp", 0),), 1, False)
        return advance(
            fields, mobility, padded[:, :-1], padded[:, -1], layered[:-2], layered[2:], driving_term
        )

    band_width = cols_total // col_parts
    fold_factor = 1.0
    band_part = band_width // row_parts
    band_freqs = col_place * band_width + jnp.arange(band_width, dtype=jnp.int32)
    held_freqs = (
        col_place * band_width + row_place * band_part + jnp.arange(band_part, dtype=jnp.int32)
    )
    held_cols = col_place * tile_cols + jnp.arange(tile_cols, dtype=jnp.int32)
    row_freqs = jnp.arange(rows_total, dtype=jnp.int32)
    tables = row_tables(rows_total)
    unit_row, unit_col = directions(row_freqs[None, :], held_freqs[:, None], rows_total, cols_total)
    middle = step_fields(order_field, 0.0)
    eigen_field = jnp.einsum("lixy,ic->lcxy", middle * middle, eigen_strain, precision=PRECISE)
    strain = jnp.broadcast_to(macro_strain[None, :, None, None], eigen_field.shape)
    for sweep_index in range(ITERS):
        stress = stress_of(strain, eigen_field, lambda_cell, shear_cell)
        flat_stress = stress.reshape(batch_size, tile_rows, tile_cols)
        empty_forward = jnp.zeros((batch_size, row_parts, band_part, tile_rows), jnp.float32)
        section = lax.all_gather(flat_stress, "col", axis=2, tiled=True)
        forward_extent = section.shape[2]
        col_ids = jnp.arange(forward_extent, dtype=jnp.int32)
        forward_cosine, forward_sine = twiddle(col_ids, band_freqs, cols_total)
        forward_cosine = forward_cosine.reshape(forward_extent, row_parts, band_part)
        forward_sine = forward_sine.reshape(forward_extent, row_parts, band_part)
        real_sum = jnp.einsum("nrx,xbq->nbqr", section, forward_cosine, precision=PRECISE)
        imag_sum = (empty_forward, empty_forward)[1] - jnp.einsum(
            "nrx,xbq->nbqr", section, forward_sine, precision=PRECISE
        )
        real_sum, imag_sum = (real_sum, imag_sum)
        real_recv, imag_recv = (
            lax.all_to_all(
                real_sum.reshape(batch_size, row_parts, band_part * tile_rows),
                "row",
                split_axis=1,
                concat_axis=1,
                tiled=True,
            ),
            lax.all_to_all(
                imag_sum.reshape(batch_size, row_parts, band_part * tile_rows),
                "row",
                split_axis=1,
                concat_axis=1,
                tiled=True,
            ),
        )
        real_rows = jnp.transpose(
            real_recv.reshape(batch_size, row_parts, band_part, tile_rows), (0, 2, 1, 3)
        ).reshape(batch_size, band_part, rows_total)
        imag_rows = jnp.transpose(
            imag_recv.reshape(batch_size, row_parts, band_part, tile_rows), (0, 2, 1, 3)
        ).reshape(batch_size, band_part, rows_total)
        spec_real, spec_imag = row_transform(real_rows, imag_rows, tables, -1.0)
        spec_real = spec_real.reshape(layer_count, 3, band_part, rows_total)
        spec_imag = spec_imag.reshape(layer_count, 3, band_part, rows_total)
        green_real = jnp.stack(
            green(spec_real[:, 0], spec_real[:, 1], spec_real[:, 2], unit_row, unit_col), axis=1
        ).reshape(batch_size, band_part, rows_total)
        green_imag = jnp.stack(
            green(spec_imag[:, 0], spec_imag[:, 1], spec_imag[:, 2], unit_row, unit_col), axis=1
        ).reshape(batch_size, band_part, rows_total)
        back_real, back_imag = row_transform(green_real, green_imag, tables, 1.0)
        back_real = jnp.transpose(
            back_real.reshape(batch_size, band_part, row_parts, tile_rows), (0, 2, 1, 3)
        )
        back_imag = jnp.transpose(
            back_imag.reshape(batch_size, band_part, row_parts, tile_rows), (0, 2, 1, 3)
        )
        back_real, back_imag = (
            lax.all_to_all(
                back_real.reshape(batch_size, row_parts, band_part * tile_rows),
                "row",
                split_axis=1,
                concat_axis=1,
                tiled=True,
            ),
            lax.all_to_all(
                back_imag.reshape(batch_size, row_parts, band_part * tile_rows),
                "row",
                split_axis=1,
                concat_axis=1,
                tiled=True,
            ),
        )
        back_real = back_real.reshape(batch_size, band_width, tile_rows)
        back_imag = back_imag.reshape(batch_size, band_width, tile_rows)
        sections = (
            lax.all_gather(back_real, "col", axis=1, tiled=True),
            lax.all_gather(back_imag, "col", axis=1, tiled=True),
        )
        extent = sections[0].shape[1]
        freq_ids = jnp.arange(extent, dtype=jnp.int32)
        cosine, sine = twiddle(freq_ids, held_cols, cols_total)
        factor = jnp.where(freq_ids == 0, 1.0, fold_factor)[:, None]
        totals = jnp.einsum("nkr,ky->nry", sections[0], cosine * factor, precision=PRECISE)
        summed = totals - jnp.einsum("nkr,ky->nry", sections[1], sine * factor, precision=PRECISE)
        correction = summed.reshape(layer_count, 3, tile_rows, tile_cols) / (
            rows_total * cols_total
        )
        strain = strain - correction
    stress = stress_of(strain, eigen_field, lambda_cell, shear_cell)
    updated = step_fields(middle, driving(stress, middle, eigen_strain))
    return (updated, strain)


def solution(mesh):
    return jax.shard_map(
        body,
        mesh=mesh,
        in_specs=(
            P("grp", None, "row", "col"),
            P("grp", "row", "col"),
            P("grp", "row", "col"),
            P(),
            P(),
            P(),
            P(),
            P(),
        ),
        out_specs=(P("grp", None, "row", "col"), P("grp", None, "row", "col")),
        check_vma=False,
    )
```

profile of v0, /device:TPU:7, one launch (start us, length us, event | category | flops | bytes accessed | tf_op | source)
XLA Modules:
  0.0 574.6 jit_solution(14822000402433748874)
XLA Ops:
  16.3 7.5 %collective-permute-start.5 = (f32[1,16,32,512]{3,1,2,0:T(8,128)}, f32[1,16,32,512]{3,1,2,0:T(8,128)}, u32[]{:S(2)}, u32[]{:S(2)}) collective-permute-start(f32[1,16,32,512]{3,1,2,0:T(8,128)} %get-tuple-element.35), channel_id=1, source_target_pairs={{64,0},{65,1},{66,2},{67,3},{68,4},{69,5},{70,6},{71,7},{72,8},{73... | collective-permute-start | bytes 3145736 | tf_op jit(solution)/shard_map/ppermute | solution.py:29
  62.9 13.8 %subtract_bitcast_fusion.5 = f32[6,32,16,32]{3,2,0,1:T(8,128)} fusion(s32[32,16]{1,0:T(8,128)S(1)} %copy-done.58, f32[6,32,1024]{2,1,0:T(8,128)S(1)} %all_gather.18), kind=kOutput, calls=%fused_computation.185 | convolution fusion | flops 1215397888 | bytes 1181696 | tf_op jit(solution)/shard_map/nrx,xbq->nbqr/dot_general | solution.py:216
  76.7 14.0 %fusion.149 = f32[6,32,16,32]{3,2,0,1:T(8,128)} fusion(s32[32,16]{1,0:T(8,128)S(1)} %copy-done.58, f32[6,32,1024]{2,1,0:T(8,128)S(1)} %all_gather.18), kind=kOutput, calls=%fused_computation.186 | convolution fusion | flops 1215299584 | bytes 1181696 | tf_op jit(solution)/shard_map/nrx,xbq->nbqr/dot_general | solution.py:215
  93.5 10.1 %all-to-all-start.1 = ((f32[6,32,512]{2,0,1:T(8,128)}), f32[6,32,512]{2,0,1:T(8,128)}, u32[]{:S(2)}, u32[]{:S(2)}) async-start(f32[6,32,512]{2,0,1:T(8,128)} %reshape.622), calls=%async_computation.1 | async-start | bytes 1048576 | tf_op jit(solution)/shard_map/all_to_all | solution.py:228
  115.0 8.3 %collective-permute-start.11 = (f32[1,16,32,512]{3,1,2,0:T(8,128)}, f32[1,16,32,512]{3,1,2,0:T(8,128)}, u32[]{:S(2)}, u32[]{:S(2)}) collective-permute-start(f32[1,16,32,512]{3,1,2,0:T(8,128)} %get-tuple-element.31), channel_id=1, source_target_pairs={{64,0},{65,1},{66,2},{67,3},{68,4},{69,5},{70,6},{71,7},{72,8},{73... | collective-permute-start | bytes 3145736 | tf_op jit(solution)/shard_map/ppermute | solution.py:29
  129.5 8.3 %all-to-all-start = ((f32[6,32,512]{2,0,1:T(8,128)}), f32[6,32,512]{2,0,1:T(8,128)}, u32[]{:S(2)}, u32[]{:S(2)}) async-start(f32[6,32,512]{2,0,1:T(8,128)} %reshape.620), calls=%async_computation | async-start | bytes 1048576 | tf_op jit(solution)/shard_map/all_to_all | solution.py:221
  164.1 7.4 %fusion.109 = f32[32,6,16,32]{3,0,2,1:T(8,128)S(1)} fusion(f32[32,6,16,32]{3,0,2,1:T(8,128)S(1)} %multiply_subtract_fusion.9, f32[32,6,16,32]{3,0,2,1:T(8,128)S(1)} %multiply_add_fusion.5, f32[32,32]{1,0:T(8,128)S(1)} %copy-done.45, f32[32,32]{1,0:T(8,128)S(1)} %copy.447), kind=kOutput, calls=%fused_computation.148 | convolution fusion | flops 38057984 | bytes 1187840 | tf_op jit(solution)/shard_map/...kp,pb->...bk/dot_general | solution.py:148
  171.5 8.4 %fusion.111 = f32[32,6,16,32]{3,0,2,1:T(8,128)} fusion(f32[32,6,16,32]{3,0,2,1:T(8,128)S(1)} %multiply_subtract_fusion.9, f32[32,6,16,32]{3,0,2,1:T(8,128)S(1)} %multiply_add_fusion.5, f32[32,32]{1,0:T(8,128)S(1)} %copy-done.45, f32[32,32]{1,0:T(8,128)S(1)} %copy.447), kind=kOutput, calls=%fused_computation.150 | convolution fusion | flops 38057984 | bytes 1187840 | tf_op jit(solution)/shard_map/...kp,pb->...bk/dot_general | solution.py:147
  179.9 8.4 %add_bitcast_fusion.3 = f32[6,16,32,32]{3,2,1,0:T(8,128)} fusion(f32[32,6,16,32]{3,0,2,1:T(8,128)S(1)} %fusion.109, f32[32,6,16,32]{3,0,2,1:T(8,128)S(1)} %multiply_add_fusion.5, f32[32,6,16,32]{3,0,2,1:T(8,128)S(1)} %multiply_subtract_fusion.9, f32[32,32]{1,0:T(8,128)S(1)} %copy-done.45, f32[32,32]{1,0:T(8,128)S(1)} %copy.447), kind=kOutput, calls=%fused_computation.179 | convolution fusion | flops 38254592 | bytes 1581056 | tf_op jit(solution)/shard_map/...kp,pb->...bk/dot_general | solution.py:150
  200.1 10.0 %subtract_bitcast_fusion.4 = f32[6,16,32,32]{3,2,1,0:T(8,128)} fusion(f32[32,6,16,32]{3,0,2,1:T(8,128)} %fusion.111, f32[32,6,16,32]{3,0,2,1:T(8,128)S(1)} %copy-done.2, f32[32,6,16,32]{3,0,2,1:T(8,128)S(1)} %copy-done.6, f32[32,32]{1,0:T(8,128)} %copy.448, f32[32,32]{1,0:T(8,128)S(1)} %copy.447), kind=kOutput, calls=%fused_computation.180 | convolution fusion | flops 38254592 | bytes 1581056 | tf_op jit(solution)/shard_map/...kp,pb->...bk/dot_general | solution.py:145
  231.0 8.8 %fusion.103 = f32[32,6,16,32]{3,0,2,1:T(8,128)} fusion(f32[32,6,16,32]{3,0,2,1:T(8,128)S(1)} %convolution_subtract_fusion.1, f32[32,6,16,32]{3,0,2,1:T(8,128)S(1)} %convolution_add_fusion.1, f32[32,32]{1,0:T(8,128)S(1)} %copy-done.43, f32[32,32]{1,0:T(8,128)S(1)} %copy.447), kind=kOutput, calls=%fused_computation.142 | convolution fusion | flops 38057984 | bytes 1187840 | tf_op jit(solution)/shard_map/...kp,pb->...bk/dot_general | solution.py:147
  239.9 7.3 %add_bitcast_fusion.2 = f32[6,32,16,32]{3,1,2,0:T(8,128)S(1)} fusion(f32[32,6,16,32]{3,0,2,1:T(8,128)S(1)} %fusion.101, f32[32,6,16,32]{3,0,2,1:T(8,128)S(1)} %convolution_add_fusion.1, f32[32,6,16,32]{3,0,2,1:T(8,128)S(1)} %convolution_subtract_fusion.1, f32[32,32]{1,0:T(8,128)S(1)} %copy-done.43, f32[32,32]{1,0:T(8,128)S(1)} %copy.447), kind=kOutput, calls=%fused_computation.175 | convolution fusion | flops 38156288 | bytes 1581056 | tf_op jit(solution)/shard_map/...kp,pb->...bk/dot_general | solution.py:150
  258.6 9.6 %subtract_bitcast_fusion.3 = f32[6,32,16,32]{3,1,2,0:T(8,128)S(1)} fusion(f32[32,6,16,32]{3,0,2,1:T(8,128)} %fusion.103, f32[32,6,16,32]{3,0,2,1:T(8,128)} %copy-done.10, f32[32,6,16,32]{3,0,2,1:T(8,128)} %copy-done.12, f32[32,32]{1,0:T(8,128)} %copy.449, f32[32,32]{1,0:T(8,128)S(1)} %copy.447), kind=kOutput, calls=%fused_computation.176 | convolution fusion | flops 38156288 | bytes 1581056 | tf_op jit(solution)/shard_map/...kp,pb->...bk/dot_general | solution.py:145
  273.1 7.9 %all-to-all-start.2 = ((f32[6,32,512]{2,0,1:T(8,128)}), f32[6,32,512]{2,0,1:T(8,128)}, u32[]{:S(2)}, u32[]{:S(2)}) async-start(f32[6,32,512]{2,0,1:T(8,128)} %reshape.624), calls=%async_computation.2 | async-start | bytes 1048576 | tf_op jit(solution)/shard_map/all_to_all | solution.py:259
  306.4 10.9 %fusion.65 = f32[6,32,512]{2,1,0:T(8,128)S(1)} fusion(f32[6,1024,32]{1,2,0:T(8,128)} %all_gather.20, s32[512]{0:T(512)S(1)} %iota_add_fusion), kind=kOutput, calls=%fused_computation.104 | convolution fusion | flops 1215299584 | bytes 1181696 | tf_op jit(solution)/shard_map/nkr,ky->nry/dot_general | solution.py:285
  317.4 9.5 %fusion.170 = f32[6,32,512]{2,1,0:T(8,128)S(1)} fusion(f32[6,32,512]{2,1,0:T(8,128)S(1)} %fusion.65, f32[6,1024,32]{1,2,0:T(8,128)S(1)} %all_gather.19, s32[512]{0:T(512)S(1)} %iota_add_fusion), kind=kOutput, calls=%fused_computation.201 | convolution fusion | flops 1215496192 | bytes 1574912 | tf_op jit(solution)/shard_map/nkr,ky->nry/dot_general | solution.py:284
  330.9 14.3 %subtract_bitcast_fusion.2 = f32[6,32,16,32]{3,2,0,1:T(8,128)} fusion(s32[32,16]{1,0:T(8,128)S(1)} %copy-done.59, f32[6,32,1024]{2,1,0:T(8,128)S(1)} %all_gather.21), kind=kOutput, calls=%fused_computation.174 | convolution fusion | flops 1215397888 | bytes 1181696 | tf_op jit(solution)/shard_map/nrx,xbq->nbqr/dot_general | solution.py:216
  348.0 7.8 %all-to-all-start.5 = ((f32[6,32,512]{2,0,1:T(8,128)}), f32[6,32,512]{2,0,1:T(8,128)}, u32[]{:S(2)}, u32[]{:S(2)}) async-start(f32[6,32,512]{2,0,1:T(8,128)} %reshape.628), calls=%async_computation.5 | async-start | bytes 1048576 | tf_op jit(solution)/shard_map/all_to_all | solution.py:228
  355.8 14.9 %fusion.152 = f32[6,32,16,32]{3,2,0,1:T(8,128)} fusion(s32[32,16]{1,0:T(8,128)} %add_add_fusion, f32[6,32,1024]{2,1,0:T(8,128)} %copy-done.47), kind=kOutput, calls=%fused_computation.187 | convolution fusion | flops 1215299584 | bytes 1181696 | tf_op jit(solution)/shard_map/nrx,xbq->nbqr/dot_general | solution.py:215
  373.5 7.9 %all-to-all-start.4 = ((f32[6,32,512]{2,0,1:T(8,128)}), f32[6,32,512]{2,0,1:T(8,128)}, u32[]{:S(2)}, u32[]{:S(2)}) async-start(f32[6,32,512]{2,0,1:T(8,128)} %reshape.626), calls=%async_computation.4 | async-start | bytes 1048576 | tf_op jit(solution)/shard_map/all_to_all | solution.py:221
  401.9 7.4 %fusion.85 = f32[32,6,16,32]{3,0,2,1:T(8,128)S(1)} fusion(f32[32,6,16,32]{3,0,2,1:T(8,128)S(1)} %multiply_subtract_fusion.6, f32[32,6,16,32]{3,0,2,1:T(8,128)S(1)} %multiply_add_fusion.2, f32[32,32]{1,0:T(8,128)S(1)} %copy-done.46, f32[32,32]{1,0:T(8,128)S(1)} %copy.447), kind=kOutput, calls=%fused_computation.124 | convolution fusion | flops 38057984 | bytes 1187840 | tf_op jit(solution)/shard_map/...kp,pb->...bk/dot_general | solution.py:148
  409.3 8.4 %fusion.87 = f32[32,6,16,32]{3,0,2,1:T(8,128)} fusion(f32[32,6,16,32]{3,0,2,1:T(8,128)S(1)} %multiply_subtract_fusion.6, f32[32,6,16,32]{3,0,2,1:T(8,128)S(1)} %multiply_add_fusion.2, f32[32,32]{1,0:T(8,128)S(1)} %copy-done.46, f32[32,32]{1,0:T(8,128)S(1)} %copy.447), kind=kOutput, calls=%fused_computation.126 | convolution fusion | flops 38057984 | bytes 1187840 | tf_op jit(solution)/shard_map/...kp,pb->...bk/dot_general | solution.py:147
  417.7 8.4 %add_bitcast_fusion.1 = f32[6,16,32,32]{3,2,1,0:T(8,128)} fusion(f32[32,6,16,32]{3,0,2,1:T(8,128)S(1)} %fusion.85, f32[32,6,16,32]{3,0,2,1:T(8,128)S(1)} %multiply_add_fusion.2, f32[32,6,16,32]{3,0,2,1:T(8,128)S(1)} %multiply_subtract_fusion.6, f32[32,32]{1,0:T(8,128)S(1)} %copy-done.46, f32[32,32]{1,0:T(8,128)S(1)} %copy.447), kind=kOutput, calls=%fused_computation.168 | convolution fusion | flops 38254592 | bytes 1581056 | tf_op jit(solution)/shard_map/...kp,pb->...bk/dot_general | solution.py:150
  437.9 10.2 %subtract_bitcast_fusion.1 = f32[6,16,32,32]{3,2,1,0:T(8,128)} fusion(f32[32,6,16,32]{3,0,2,1:T(8,128)} %fusion.87, f32[32,6,16,32]{3,0,2,1:T(8,128)S(1)} %copy-done.4, f32[32,6,16,32]{3,0,2,1:T(8,128)S(1)} %copy-done.8, f32[32,32]{1,0:T(8,128)} %copy.448, f32[32,32]{1,0:T(8,128)S(1)} %copy.447), kind=kOutput, calls=%fused_computation.169 | convolution fusion | flops 38254592 | bytes 1581056 | tf_op jit(solution)/shard_map/...kp,pb->...bk/dot_general | solution.py:145
  461.8 7.2 %fusion.77 = f32[32,6,16,32]{3,0,2,1:T(8,128)S(1)} fusion(f32[32,6,16,32]{3,0,2,1:T(8,128)S(1)} %convolution_subtract_fusion, f32[32,6,16,32]{3,0,2,1:T(8,128)S(1)} %convolution_add_fusion, f32[32,32]{1,0:T(8,128)S(1)} %copy-done.44, f32[32,32]{1,0:T(8,128)S(1)} %copy.447), kind=kOutput, calls=%fused_computation.116 | convolution fusion | flops 38057984 | bytes 1187840 | tf_op jit(solution)/shard_map/...kp,pb->...bk/dot_general | solution.py:148
  469.1 8.6 %fusion.79 = f32[32,6,16,32]{3,0,2,1:T(8,128)} fusion(f32[32,6,16,32]{3,0,2,1:T(8,128)S(1)} %convolution_subtract_fusion, f32[32,6,16,32]{3,0,2,1:T(8,128)S(1)} %convolution_add_fusion, f32[32,32]{1,0:T(8,128)S(1)} %copy-done.44, f32[32,32]{1,0:T(8,128)S(1)} %copy.447), kind=kOutput, calls=%fused_computation.118 | convolution fusion | flops 38057984 | bytes 1187840 | tf_op jit(solution)/shard_map/...kp,pb->...bk/dot_general | solution.py:147
  477.6 7.3 %add_bitcast_fusion = f32[6,32,16,32]{3,1,2,0:T(8,128)S(1)} fusion(f32[32,6,16,32]{3,0,2,1:T(8,128)S(1)} %fusion.77, f32[32,6,16,32]{3,0,2,1:T(8,128)S(1)} %convolution_add_fusion, f32[32,6,16,32]{3,0,2,1:T(8,128)S(1)} %convolution_subtract_fusion, f32[32,32]{1,0:T(8,128)S(1)} %copy-done.44, f32[32,32]{1,0:T(8,128)S(1)} %copy.447), kind=kOutput, calls=%fused_computation.164 | convolution fusion | flops 38156288 | bytes 1581056 | tf_op jit(solution)/shard_map/...kp,pb->...bk/dot_general | solution.py:150
  489.7 8.2 %all-to-all-start.7 = ((f32[6,32,512]{2,0,1:T(8,128)}), f32[6,32,512]{2,0,1:T(8,128)}, u32[]{:S(2)}, u32[]{:S(2)}) async-start(f32[6,32,512]{2,0,1:T(8,128)} %reshape.631), calls=%async_computation.7 | async-start | bytes 1048576 | tf_op jit(solution)/shard_map/all_to_all | solution.py:266
  497.9 9.6 %subtract_bitcast_fusion = f32[6,32,16,32]{3,1,2,0:T(8,128)S(1)} fusion(f32[32,6,16,32]{3,0,2,1:T(8,128)} %fusion.79, f32[32,6,16,32]{3,0,2,1:T(8,128)} %copy-done.9, f32[32,6,16,32]{3,0,2,1:T(8,128)} %copy-done.11, f32[32,32]{1,0:T(8,128)S(1)} %copy-done.44, f32[32,32]{1,0:T(8,128)S(1)} %copy.447), kind=kOutput, calls=%fused_computation.165 | convolution fusion | flops 38156288 | bytes 1581056 | tf_op jit(solution)/shard_map/...kp,pb->...bk/dot_general | solution.py:145
  512.3 7.8 %all-to-all-start.6 = ((f32[6,32,512]{2,0,1:T(8,128)}), f32[6,32,512]{2,0,1:T(8,128)}, u32[]{:S(2)}, u32[]{:S(2)}) async-start(f32[6,32,512]{2,0,1:T(8,128)} %reshape.630), calls=%async_computation.6 | async-start | bytes 1048576 | tf_op jit(solution)/shard_map/all_to_all | solution.py:259
  531.9 10.3 %fusion.63 = f32[6,32,512]{2,1,0:T(8,128)} fusion(f32[6,1024,32]{1,2,0:T(8,128)S(1)} %all_gather.23, s32[512]{0:T(512)S(1)} %iota_add_fusion), kind=kOutput, calls=%fused_computation.102 | convolution fusion | flops 1215299584 | bytes 1181696 | tf_op jit(solution)/shard_map/nkr,ky->nry/dot_general | solution.py:285
  552.0 10.7 %fusion.176 = f32[6,32,512]{2,1,0:T(8,128)S(1)} fusion(f32[6,32,512]{2,1,0:T(8,128)} %fusion.63, f32[6,1024,32]{1,2,0:T(8,128)S(1)} %all_gather.22, s32[512]{0:T(512)S(1)} %iota_add_fusion), kind=kOutput, calls=%fused_computation.203 | convolution fusion | flops 1215496192 | bytes 1574912 | tf_op jit(solution)/shard_map/nkr,ky->nry/dot_general | solution.py:284
  (282 shorter events, 273.0 us)
Async XLA Ops:
  0.6 56.1 %copy-start = (f32[16,3]{0,1:T(4,128)S(1)}, f32[16,3]{0,1:T(4,128)}, u32[]{:S(2)}) copy-start(f32[16,3]{0,1:T(4,128)} %param.14) | copy-start | bytes 580
  2.1 42.3 %copy-start.33 = (f32[2,32,512]{2,1,0:T(8,128)}, f32[2,32,512]{2,1,0:T(8,128)S(1)}, u32[]{:S(2)}) copy-start(f32[2,32,512]{2,1,0:T(8,128)S(1)} %select_reduce_fusion) | copy-start | bytes 393220
  2.2 48.2 %copy-start.30 = (f32[2,1,32,512]{3,1,2,0:T(1,128)}, f32[2,1,32,512]{3,1,2,0:T(1,128)S(1)}, u32[]{:S(2)}) copy-start(f32[2,1,32,512]{3,1,2,0:T(1,128)S(1)} %broadcast_in_dim.66) | copy-start | bytes 393220
  11.3 15.3 %collective-permute-start = (f32[2,17,1,512]{3,1,2,0:T(8,128)S(1)}, f32[2,17,1,512]{3,1,2,0:T(8,128)S(1)}, u32[]{:S(2)}, u32[]{:S(2)}) collective-permute-start(f32[2,17,1,512]{3,1,2,0:T(8,128)S(1)} %get-tuple-element.24), channel_id=1, source_target_pairs={{0,2},{2,4},{4,6},{6,8},{8,10},{10,12},{12,14},{14,16},{16,18},{18... | collective-permute-start | bytes 208904 | tf_op jit(solution)/shard_map/ppermute | solution.py:28
  13.3 13.4 %collective-permute-start.1 = (f32[2,17,1,512]{3,1,2,0:T(8,128)S(1)}, f32[2,17,1,512]{3,1,2,0:T(8,128)S(1)}, u32[]{:S(2)}, u32[]{:S(2)}) collective-permute-start(f32[2,17,1,512]{3,1,2,0:T(8,128)S(1)} %get-tuple-element.25), channel_id=1, source_target_pairs={{2,0},{4,2},{6,4},{8,6},{10,8},{12,10},{14,12},{16,14},{18,16},{20... | collective-permute-start | bytes 208904 | tf_op jit(solution)/shard_map/ppermute | solution.py:29
  13.3 11.4 %copy-start.53 = (s32[2,32,512]{2,1,0:T(8,128)S(1)}, s32[2,32,512]{2,1,0:T(8,128)}, u32[]{:S(2)}) copy-start(s32[2,32,512]{2,1,0:T(8,128)} %param.10) | copy-start | bytes 393220
  15.0 27.4 %collective-permute-start.4 = (f32[1,16,32,512]{3,1,2,0:T(8,128)}, f32[1,16,32,512]{3,1,2,0:T(8,128)}, u32[]{:S(2)}, u32[]{:S(2)}) collective-permute-start(f32[1,16,32,512]{3,1,2,0:T(8,128)} %get-tuple-element.34), channel_id=1, source_target_pairs={{0,64},{1,65},{2,66},{3,67},{4,68},{5,69},{6,70},{7,71},{8,72},{9,... | collective-permute-start | bytes 3145736 | tf_op jit(solution)/shard_map/ppermute | solution.py:28
  16.3 28.0 %collective-permute-start.5 = (f32[1,16,32,512]{3,1,2,0:T(8,128)}, f32[1,16,32,512]{3,1,2,0:T(8,128)}, u32[]{:S(2)}, u32[]{:S(2)}) collective-permute-start(f32[1,16,32,512]{3,1,2,0:T(8,128)} %get-tuple-element.35), channel_id=1, source_target_pairs={{64,0},{65,1},{66,2},{67,3},{68,4},{69,5},{70,6},{71,7},{72,8},{73... | collective-permute-start | bytes 3145736 | tf_op jit(solution)/shard_map/ppermute | solution.py:29
  29.2 3.6 collective-permute-start.3
  30.8 1.5 collective-permute-start.2
  51.1 52.5 %collective-permute-start.6 = (f32[2,17,1,512]{3,1,2,0:T(8,128)}, f32[2,17,1,512]{3,1,2,0:T(8,128)}, u32[]{:S(2)}, u32[]{:S(2)}) collective-permute-start(f32[2,17,1,512]{3,1,2,0:T(8,128)} %get-tuple-element.28), channel_id=1, source_target_pairs={{0,2},{2,4},{4,6},{6,8},{8,10},{10,12},{12,14},{14,16},{16,18},{18... | collective-permute-start | bytes 208904 | tf_op jit(solution)/shard_map/ppermute | solution.py:28
  53.1 50.4 %collective-permute-start.7 = (f32[2,17,1,512]{3,1,2,0:T(8,128)}, f32[2,17,1,512]{3,1,2,0:T(8,128)}, u32[]{:S(2)}, u32[]{:S(2)}) collective-permute-start(f32[2,17,1,512]{3,1,2,0:T(8,128)} %get-tuple-element.29), channel_id=1, source_target_pairs={{2,0},{4,2},{6,4},{8,6},{10,8},{12,10},{14,12},{16,14},{18,16},{20... | collective-permute-start | bytes 208904 | tf_op jit(solution)/shard_map/ppermute | solution.py:29
  93.5 36.0 %all-to-all-start.1 = ((f32[6,32,512]{2,0,1:T(8,128)}), f32[6,32,512]{2,0,1:T(8,128)}, u32[]{:S(2)}, u32[]{:S(2)}) async-start(f32[6,32,512]{2,0,1:T(8,128)} %reshape.622), calls=%async_computation.1 | async-start | bytes 1048576 | tf_op jit(solution)/shard_map/all_to_all | solution.py:228
  108.7 15.8 %collective-permute-start.9 = (f32[2,17,34,1]{2,0,3,1:T(2,128)}, f32[2,17,34,1]{2,0,3,1:T(2,128)}, u32[]{:S(2)}, u32[]{:S(2)}) collective-permute-start(f32[2,17,34,1]{2,0,3,1:T(2,128)} %copy.428), channel_id=1, source_target_pairs={{1,0},{0,1},{3,2},{2,3},{5,4},{4,5},{7,6},{6,7},{9,8},{8,9},{11,10... | collective-permute-start | bytes 13880 | tf_op jit(solution)/shard_map/ppermute | solution.py:29
  109.3 14.0 %collective-permute-start.8 = (f32[2,17,34,1]{2,0,3,1:T(2,128)}, f32[2,17,34,1]{2,0,3,1:T(2,128)}, u32[]{:S(2)}, u32[]{:S(2)}) collective-permute-start(f32[2,17,34,1]{2,0,3,1:T(2,128)} %copy.427), channel_id=1, source_target_pairs={{0,1},{1,0},{2,3},{3,2},{4,5},{5,4},{6,7},{7,6},{8,9},{9,8},{10,11... | collective-permute-start | bytes 13880 | tf_op jit(solution)/shard_map/ppermute | solution.py:28
  113.7 452.1 %collective-permute-start.10 = (f32[1,16,32,512]{3,1,2,0:T(8,128)}, f32[1,16,32,512]{3,1,2,0:T(8,128)}, u32[]{:S(2)}, u32[]{:S(2)}) collective-permute-start(f32[1,16,32,512]{3,1,2,0:T(8,128)} %get-tuple-element.30), channel_id=1, source_target_pairs={{0,64},{1,65},{2,66},{3,67},{4,68},{5,69},{6,70},{7,71},{8,72},{9,... | collective-permute-start | bytes 3145736 | tf_op jit(solution)/shard_map/ppermute | solution.py:28
  115.0 450.8 %collective-permute-start.11 = (f32[1,16,32,512]{3,1,2,0:T(8,128)}, f32[1,16,32,512]{3,1,2,0:T(8,128)}, u32[]{:S(2)}, u32[]{:S(2)}) collective-permute-start(f32[1,16,32,512]{3,1,2,0:T(8,128)} %get-tuple-element.31), channel_id=1, source_target_pairs={{64,0},{65,1},{66,2},{67,3},{68,4},{69,5},{70,6},{71,7},{72,8},{73... | collective-permute-start | bytes 3145736 | tf_op jit(solution)/shard_map/ppermute | solution.py:29
  129.5 25.2 %all-to-all-start = ((f32[6,32,512]{2,0,1:T(8,128)}), f32[6,32,512]{2,0,1:T(8,128)}, u32[]{:S(2)}, u32[]{:S(2)}) async-start(f32[6,32,512]{2,0,1:T(8,128)} %reshape.620), calls=%async_computation | async-start | bytes 1048576 | tf_op jit(solution)/shard_map/all_to_all | solution.py:221
  161.6 18.2 %copy-start.1 = (f32[32,6,16,32]{3,0,2,1:T(8,128)}, f32[32,6,16,32]{3,0,2,1:T(8,128)S(1)}, u32[]{:S(2)}) copy-start(f32[32,6,16,32]{3,0,2,1:T(8,128)S(1)} %multiply_add_fusion.5) | copy-start | bytes 1179652
  164.1 15.8 %copy-start.5 = (f32[32,6,16,32]{3,0,2,1:T(8,128)}, f32[32,6,16,32]{3,0,2,1:T(8,128)S(1)}, u32[]{:S(2)}) copy-start(f32[32,6,16,32]{3,0,2,1:T(8,128)S(1)} %multiply_subtract_fusion.9) | copy-start | bytes 1179652
  222.2 17.6 %copy-start.10 = (f32[32,6,16,32]{3,0,2,1:T(8,128)}, f32[32,6,16,32]{3,0,2,1:T(8,128)S(1)}, u32[]{:S(2)}) copy-start(f32[32,6,16,32]{3,0,2,1:T(8,128)S(1)} %convolution_add_fusion.1) | copy-start | bytes 1179652
  223.8 16.1 %copy-start.12 = (f32[32,6,16,32]{3,0,2,1:T(8,128)}, f32[32,6,16,32]{3,0,2,1:T(8,128)S(1)}, u32[]{:S(2)}) copy-start(f32[32,6,16,32]{3,0,2,1:T(8,128)S(1)} %convolution_subtract_fusion.1) | copy-start | bytes 1179652
  251.9 21.1 %all-to-all-start.3 = ((f32[6,32,512]{2,0,1:T(8,128)}), f32[6,32,512]{2,0,1:T(8,128)}, u32[]{:S(2)}, u32[]{:S(2)}) async-start(f32[6,32,512]{2,0,1:T(8,128)} %reshape.625), calls=%async_computation.3 | async-start | bytes 1048576 | tf_op jit(solution)/shard_map/all_to_all | solution.py:266
  273.1 23.6 %all-to-all-start.2 = ((f32[6,32,512]{2,0,1:T(8,128)}), f32[6,32,512]{2,0,1:T(8,128)}, u32[]{:S(2)}, u32[]{:S(2)}) async-start(f32[6,32,512]{2,0,1:T(8,128)} %reshape.624), calls=%async_computation.2 | async-start | bytes 1048576 | tf_op jit(solution)/shard_map/all_to_all | solution.py:259
  348.0 25.5 %all-to-all-start.5 = ((f32[6,32,512]{2,0,1:T(8,128)}), f32[6,32,512]{2,0,1:T(8,128)}, u32[]{:S(2)}, u32[]{:S(2)}) async-start(f32[6,32,512]{2,0,1:T(8,128)} %reshape.628), calls=%async_computation.5 | async-start | bytes 1048576 | tf_op jit(solution)/shard_map/all_to_all | solution.py:228
  373.5 19.0 %all-to-all-start.4 = ((f32[6,32,512]{2,0,1:T(8,128)}), f32[6,32,512]{2,0,1:T(8,128)}, u32[]{:S(2)}, u32[]{:S(2)}) async-start(f32[6,32,512]{2,0,1:T(8,128)} %reshape.626), calls=%async_computation.4 | async-start | bytes 1048576 | tf_op jit(solution)/shard_map/all_to_all | solution.py:221
  399.5 18.3 %copy-start.3 = (f32[32,6,16,32]{3,0,2,1:T(8,128)}, f32[32,6,16,32]{3,0,2,1:T(8,128)S(1)}, u32[]{:S(2)}) copy-start(f32[32,6,16,32]{3,0,2,1:T(8,128)S(1)} %multiply_add_fusion.2) | copy-start | bytes 1179652
  401.9 15.8 %copy-start.7 = (f32[32,6,16,32]{3,0,2,1:T(8,128)}, f32[32,6,16,32]{3,0,2,1:T(8,128)S(1)}, u32[]{:S(2)}) copy-start(f32[32,6,16,32]{3,0,2,1:T(8,128)S(1)} %multiply_subtract_fusion.6) | copy-start | bytes 1179652
  460.3 17.4 %copy-start.9 = (f32[32,6,16,32]{3,0,2,1:T(8,128)}, f32[32,6,16,32]{3,0,2,1:T(8,128)S(1)}, u32[]{:S(2)}) copy-start(f32[32,6,16,32]{3,0,2,1:T(8,128)S(1)} %convolution_add_fusion) | copy-start | bytes 1179652
  461.8 15.8 %copy-start.11 = (f32[32,6,16,32]{3,0,2,1:T(8,128)}, f32[32,6,16,32]{3,0,2,1:T(8,128)S(1)}, u32[]{:S(2)}) copy-start(f32[32,6,16,32]{3,0,2,1:T(8,128)S(1)} %convolution_subtract_fusion) | copy-start | bytes 1179652
  489.7 22.6 %all-to-all-start.7 = ((f32[6,32,512]{2,0,1:T(8,128)}), f32[6,32,512]{2,0,1:T(8,128)}, u32[]{:S(2)}, u32[]{:S(2)}) async-start(f32[6,32,512]{2,0,1:T(8,128)} %reshape.631), calls=%async_computation.7 | async-start | bytes 1048576 | tf_op jit(solution)/shard_map/all_to_all | solution.py:266
  512.3 29.9 %all-to-all-start.6 = ((f32[6,32,512]{2,0,1:T(8,128)}), f32[6,32,512]{2,0,1:T(8,128)}, u32[]{:S(2)}, u32[]{:S(2)}) async-start(f32[6,32,512]{2,0,1:T(8,128)} %reshape.630), calls=%async_computation.6 | async-start | bytes 1048576 | tf_op jit(solution)/shard_map/all_to_all | solution.py:259
  (51 other events, 236.9 us)
where the time goes:
time: 585 us; the launch traced here: 575 us
  matrix products  287 us (49%)
  local copies, waits for them, and re-layouts  120 us (21%)
  starting transfers between devices  93 us (16%)
  other arithmetic  35.6 us (6%)
  blocking collectives  23.2 us (4%)
  waiting for transfers between devices  14.1 us (2%)
    dot_general x4, matrix products, row_transform(): jnp.einsum('...kp,pb->...bk', turned_real, last_cos, precision=PRECISE)  39.5 us
    dot_general x4, matrix products, row_transform(): jnp.einsum('...kp,pb->...bk', turned_imag, last_sin, precision=PRECISE)  34.2 us
    dot_general x4, matrix products, row_transform(): jnp.einsum('...kp,pb->...bk', turned_real, last_sin, precision=PRECISE)  31.4 us
    dot_general x4, matrix products, row_transform(): jnp.einsum('...kp,pb->...bk', turned_imag, last_cos, precision=PRECISE)  29.3 us
    dot_general x2, matrix products, body(): jnp.einsum('nrx,xbq->nbqr', section, forward_cosine, precision=PRECISE)  28.9 us
    dot_general x2, matrix products, body(): jnp.einsum('nrx,xbq->nbqr', section, forward_sine, precision=PRECISE)  28.1 us
    ppermute x6, starting transfers between devices, with_halo(): after = lax.ppermute(initial, axis, down)  21.6 us
    dot_general x2, matrix products, body(): jnp.einsum('nkr,ky->nry', sections[1], sine * factor, precision=PRECISE)  21.2 us
  transfers between devices with their start and end apart: 20, of which 3 were waited for; matrix products, arithmetic and copies ran while one was open for 72% of the time, Pallas kernels for 0%

commit v1 on v0

v1 whole, which is shorter than its diff:
```python
import jax
import jax.numpy as jnp
import ml_dtypes
import numpy as np
from jax import lax
from jax.experimental import pallas as pl
from jax.experimental.pallas import tpu as pltpu
from jax.sharding import PartitionSpec as P

MESH = pl.DeviceIdType.MESH
ITERS = 2
ROWS = 32
HALF = 0.7071067811865476
LAMBDA_REF = 1.25
SHEAR_REF = 1.25
BETA_REF = (LAMBDA_REF + SHEAR_REF) / (SHEAR_REF * (LAMBDA_REF + 2.0 * SHEAR_REF))
F32 = jnp.float32
BF16 = jnp.bfloat16
CHUNK = 4
CHUNKS = 16 // CHUNK


def split_table(values):
    high = values.astype(np.float32).astype(ml_dtypes.bfloat16)
    low = (values - high.astype(np.float64)).astype(np.float32).astype(ml_dtypes.bfloat16)
    return high, low


def tables():
    place = np.arange(128, dtype=np.float64)
    forward = np.zeros((4, 256, 256))
    inverse = np.zeros((4, 256, 256))
    scale = 1.0 / 1048576.0
    half = np.arange(64, dtype=np.float64)
    for first, base in ((0, 0), (64, 4)):
        angle = 2.0 * np.pi * np.outer(base + 8 * half, place) / 1024.0
        source = slice(0, 128) if base == 0 else slice(128, 256)
        forward[0, first : first + 64, source] = np.cos(angle)
        forward[0, 128 + first : 192 + first, source] = -np.sin(angle)
        weight = np.full((64, 1), 2.0 * scale)
        if base == 0:
            weight[0] = scale
        inverse[0, source, first : first + 64] = (weight * np.cos(angle)).T
        inverse[0, source, 128 + first : 192 + first] = (-weight * np.sin(angle)).T
    for kind in (1, 2, 3):
        angle = 2.0 * np.pi * np.outer(kind + 8 * place, place) / 1024.0
        cosine, sine = np.cos(angle), np.sin(angle)
        forward[kind] = np.block([[cosine, sine], [-sine, cosine]])
        inverse[kind] = 2.0 * scale * np.block([[cosine.T, -sine.T], [sine.T, cosine.T]])
    small = np.arange(32, dtype=np.float64)
    angle = 2.0 * np.pi * np.outer(small, small) / 32.0
    cosine, sine = np.kron(np.eye(4), np.cos(angle)), np.kron(np.eye(4), np.sin(angle))
    rows_forward = np.block([[cosine, -sine], [sine, cosine]])
    rows_inverse = np.block([[cosine, sine], [-sine, cosine]])
    angle = 2.0 * np.pi * np.outer(small, np.tile(small, 4)) / 1024.0
    turn = np.stack([np.cos(angle), np.sin(angle)], axis=1).astype(np.float32)
    return (
        split_table(forward)
        + split_table(inverse)
        + split_table(rows_forward)
        + split_table(rows_inverse)
        + (turn,)
    )


def times(value, angle_index, length, sign):
    real, imag = value
    angle_index = angle_index % length
    if angle_index == 0:
        return value
    angle = 2.0 * np.pi * angle_index / length
    cosine, sine = float(np.cos(angle)), float(sign * np.sin(angle))
    if 4 * angle_index == length or 4 * angle_index == 3 * length:
        return (-imag, real) if sine > 0 else (imag, -real)
    if 2 * angle_index == length:
        return (-real, -imag)
    return (real * cosine - imag * sine, imag * cosine + real * sine)


def plus(first, second):
    return (first[0] + second[0], first[1] + second[1])


def minus(first, second):
    return (first[0] - second[0], first[1] - second[1])


def four(x, sign):
    a, b, c, d = plus(x[0], x[2]), minus(x[0], x[2]), plus(x[1], x[3]), minus(x[1], x[3])
    d = (-d[1], d[0]) if sign > 0 else (d[1], -d[0])
    return [plus(a, c), plus(b, d), minus(a, c), minus(b, d)]


def eight(x, sign):
    even, odd = four(x[0::2], sign), four(x[1::2], sign)
    odd = [odd[0], times(odd[1], 1, 8, sign), times(odd[2], 2, 8, sign), times(odd[3], 3, 8, sign)]
    return [plus(e, o) for e, o in zip(even, odd)] + [minus(e, o) for e, o in zip(even, odd)]


def parts(value):
    high = value.astype(BF16)
    return high, (value - high.astype(F32)).astype(BF16)


def dot(a, b):
    return jnp.dot(a, b, preferred_element_type=F32)


def dot3(a_high, a_low, b_high, b_low):
    return dot(a_high, b_high) + dot(a_high, b_low) + dot(a_low, b_high)


def kernel(
    order_hbm, grain_hbm, phase_hbm, tfh_hbm, tfl_hbm, tih_hbm, til_hbm, bfh_hbm, bfl_hbm, bih_hbm,
    bil_hbm, turn_hbm, mob_s, index_s, stiff_s, eigen_s, macro_s,
    out_ref, strain_ref,
    first, middle, mob, grain, phase, tfh, tfl, tih, til, bfh, bfl, bih, bil, turn,
    row_out, row_in, row_out2, row_in2, col_out, col_in, col_out2, col_in2,
    outer_in, outer_in2, lame, lame_in, eig, eig_in, final,
    strain, eig_t, m1_t, m2_t, green, send1, recv1, send2, recv2, work, high, low, flat, lxh, lxl,
    load_sem, halo_send, halo_recv, outer_send, outer_recv, core_send, core_recv, all_send, all_recv,
):
    g, r, c = lax.axis_index("grp"), lax.axis_index("row"), lax.axis_index("col")
    inner, outer = g, 1 - g
    mine = jnp.where(c == 0, inner, outer)
    other = 1 - mine
    core_peer = (g, r, 1 - c)
    grp_peer = (1 - g, r, c)
    row_up = (g, (r + ROWS - 1) % ROWS, c)
    row_down = (g, (r + 1) % ROWS, c)

    def remote(source, target, send, recv, device):
        return pltpu.make_async_remote_copy(
            source, target, send, recv, device_id=device, device_id_type=MESH
        )

    loads = [
        pltpu.make_async_copy(grain_hbm, grain, load_sem.at[0]),
        pltpu.make_async_copy(phase_hbm, phase, load_sem.at[1]),
        pltpu.make_async_copy(order_hbm, first.at[:, :, pl.ds(8, 32), :], load_sem.at[2]),
    ]
    pairs = (
        (tfh_hbm, tfh), (tfl_hbm, tfl), (tih_hbm, tih), (til_hbm, til), (bfh_hbm, bfh),
        (bfl_hbm, bfl), (bih_hbm, bih), (bil_hbm, bil), (turn_hbm, turn),
    )
    for place, (source, target) in enumerate(pairs):
        loads.append(pltpu.make_async_copy(source, target, load_sem.at[3 + place]))
    for load in loads:
        load.start()

    barrier = pltpu.get_barrier_semaphore()
    pl.semaphore_signal(barrier, inc=1, device_id=grp_peer, device_id_type=MESH)
    pl.semaphore_signal(barrier, inc=1, device_id=core_peer, device_id_type=MESH)

    def greet(step, carry):
        pl.semaphore_signal(
            barrier, inc=1, device_id=(g, (r + step) % ROWS, c), device_id_type=MESH
        )
        return carry

    lax.fori_loop(1, ROWS, greet, 0)

    loads[0].wait()
    loads[1].wait()
    for layer in range(2):
        labels = grain[layer]

        def look(k, value):
            return jnp.where(labels == k, mob_s[k], value)

        mob[layer, 8:40, :] = lax.fori_loop(0, 32, look, jnp.zeros((32, 512), F32))
        labels2 = phase[layer]

        def look2(k, values):
            chosen = index_s[k]
            hit = labels2 == k
            return (
                jnp.where(hit, stiff_s[chosen, 0], values[0]),
                jnp.where(hit, stiff_s[chosen, 1], values[1]),
            )

        empty = jnp.zeros((32, 512), F32)
        lam, shear = lax.fori_loop(0, 8, look2, (empty, empty))
        lame[layer, 0] = lam
        lame[layer, 1] = shear

    lane = lax.broadcasted_iota(jnp.int32, (32, 128), 1)

    def pack(source, rows_to, cols_to):
        def step(i, carry):
            for layer in range(2):
                k = layer * 16 + i
                rows_to[0, k] = source[layer, i, 8:9, :]
                rows_to[1, k] = source[layer, i, 39:40, :]
                cols_to[k] = jnp.where(
                    lane < 64, source[layer, i, 8:40, 0:128], source[layer, i, 8:40, 384:512]
                )
            return carry

        lax.fori_loop(0, 16, step, 0)

    def unpack(target, rows_from):
        def step(i, carry):
            for layer in range(2):
                k = layer * 16 + i
                target[layer, i, 40:41, :] = rows_from[0, k]
                target[layer, i, 7:8, :] = rows_from[1, k]
            return carry

        lax.fori_loop(0, 16, step, 0)

    loads[2].wait()
    pack(first, row_out, col_out)
    for layer in range(2):
        row_out[0, 32 + layer] = mob[layer, 8:9, :]
        row_out[1, 32 + layer] = mob[layer, 39:40, :]
        col_out[32 + layer] = jnp.where(lane < 64, mob[layer, 8:40, 0:128], mob[layer, 8:40, 384:512])

    pl.semaphore_wait(barrier, ROWS + 1)

    halo = [
        remote(row_out.at[0], row_in.at[0], halo_send.at[0], halo_recv.at[0], row_up),
        remote(row_out.at[1], row_in.at[1], halo_send.at[1], halo_recv.at[1], row_down),
        remote(col_out, col_in, halo_send.at[2], halo_recv.at[2], core_peer),
    ]
    for copy in halo:
        copy.start()

    def outer_copy(k):
        at = pl.ds(k * CHUNK, CHUNK)
        return remote(
            order_hbm.at[outer, at], outer_in.at[at], outer_send.at[k], outer_recv.at[k], grp_peer
        )

    def outer_copy2(k):
        at = pl.ds(k * CHUNK, CHUNK)
        return remote(
            middle.at[outer, at, pl.ds(8, 32), :], outer_in2.at[at],
            outer_send.at[CHUNKS + k], outer_recv.at[CHUNKS + k], grp_peer,
        )

    for k in range(CHUNKS):
        outer_copy(k).start()
    lame_copy = remote(lame.at[other], lame_in.at[c], core_send.at[0], core_recv.at[0], core_peer)
    lame_copy.start()

    sub16 = lax.broadcasted_iota(jnp.int32, (16, 128), 0)
    lane16 = lax.broadcasted_iota(jnp.int32, (16, 128), 1)
    slot = lane16 // 32
    place = (r % 8) * 16 + sub16
    kind = r // 8
    col_freq = jnp.where(
        kind > 0, kind + 8 * place, jnp.where(place < 64, 8 * place, 4 + 8 * (place - 64))
    )
    col_signed = jnp.where(col_freq >= 512, col_freq - 1024, col_freq).astype(F32)

    def green_step(k1, carry):
        row_freq = k1 + 32 * (lane16 % 32)
        row_signed = jnp.where(row_freq >= 512, row_freq - 1024, row_freq).astype(F32)
        keeper = jnp.where((row_freq != 512) & (col_freq != 512), 1.0, 0.0)
        radius = row_signed * row_signed + col_signed * col_signed
        inverse = keeper * lax.rsqrt(jnp.where(radius > 0, radius, 1.0))
        n1, n2 = row_signed * inverse, col_signed * inverse
        a, b, d = n1 * n1, n2 * n2, n1 * n2
        own = jnp.where(
            slot == 0,
            a / SHEAR_REF - BETA_REF * a * a,
            jnp.where(
                slot == 2,
                b / SHEAR_REF - BETA_REF * b * b,
                0.5 * (a + b) / SHEAR_REF - 2.0 * BETA_REF * d * d,
            ),
        )
        toward_rr = 0.5 * d / SHEAR_REF - BETA_REF * a * d
        toward_cc = 0.5 * d / SHEAR_REF - BETA_REF * b * d
        across = -BETA_REF * d * d
        green[0, k1] = own
        green[1, k1] = jnp.where(
            slot == 1, toward_cc, jnp.where(slot == 3, toward_rr, across)
        )
        green[2, k1] = jnp.where(
            slot == 0,
            2.0 * toward_rr,
            jnp.where(slot == 1, toward_rr, jnp.where(slot == 2, 2.0 * toward_cc, toward_cc)),
        )
        return carry

    lax.fori_loop(0, 32, green_step, 0)

    def to_columns(target, half, slots):
        for j in range(4):
            block = jnp.concatenate([field[:, 128 * j : 128 * j + 128] for field in slots], axis=0)
            target[4 * half + j] = block.T

    def stiff_columns(half, lam, shear):
        double = 2.0 * shear
        straight = lam + double
        to_columns(m1_t, half, (straight, double, straight, double))
        empty = jnp.zeros_like(lam)
        to_columns(m2_t, half, (lam, empty, lam, empty))

    stiff_columns(c, lame[mine, 0], lame[mine, 1])

    for copy in halo:
        copy.wait_recv()
    unpack(first, row_in)
    for layer in range(2):
        mob[layer, 40:41, :] = row_in[0, 32 + layer]
        mob[layer, 7:8, :] = row_in[1, 32 + layer]

    def update(source, cols, layer, beyond, stress, write):
        for s in range(4):
            r0, r1 = 8 + 8 * s, 8 * s
            m = mob[layer, r0 : r0 + 8, :]
            edge = jnp.concatenate([col_in[32 + layer, r1 : r1 + 8, :], m], axis=1)
            w_up = 0.05 * (m + mob[layer, r0 - 1 : r0 + 7, :])
            w_down = 0.05 * (m + mob[layer, r0 + 1 : r0 + 9, :])
            w_left = 0.05 * (m + pltpu.roll(edge, 1, 1)[:, 128:])
            w_right = 0.05 * (m + pltpu.roll(edge, 639, 1)[:, 128:])

            def square(i, total):
                v = source[layer, i, r0 : r0 + 8, :]
                return total + v * v

            total = lax.fori_loop(0, 16, square, jnp.zeros((8, 512), F32))
            c0 = 1.0 - (w_up + w_down + w_left + w_right) - 0.3 * m * total
            c1 = 0.2 * m
            m05 = 0.05 * m
            push = None if stress is None else [c1 * p for p in stress(s)]

            def step(i, carry):
                v = source[layer, i, r0 : r0 + 8, :]
                e = jnp.concatenate([cols[layer * 16 + i, r1 : r1 + 8, :], v], axis=1)
                left = pltpu.roll(e, 1, 1)[:, 128:]
                right = pltpu.roll(e, 639, 1)[:, 128:]
                near = source[1 - layer, i, r0 : r0 + 8, :]
                if beyond is not None:
                    near = near + beyond[i, r1 : r1 + 8, :]
                factor = c0 + c1 * v * v
                if push is not None:
                    factor = factor + (
                        push[0] * eigen_s[i, 0] + push[1] * eigen_s[i, 1] + push[2] * eigen_s[i, 2]
                    )
                value = (
                    v * factor
                    + w_up * source[layer, i, r0 - 1 : r0 + 7, :]
                    + w_down * source[layer, i, r0 + 1 : r0 + 9, :]
                    + w_left * left
                    + w_right * right
                    + m05 * near
                )
                write(layer, i, s, value)
                return carry

            lax.fori_loop(0, 16, step, 0)

    def to_middle(layer, i, s, value):
        middle[layer, i, 8 + 8 * s : 16 + 8 * s, :] = value

    update(first, col_in, outer, None, None, to_middle)
    update(first, col_in, inner, None, None, to_middle)

    lame_copy.wait_recv()
    stiff_columns(1 - c, lame_in[1 - c, 0], lame_in[1 - c, 1])

    for k in range(CHUNKS):
        outer_copy(k).wait_recv()

        def add(i, carry):
            j = k * CHUNK + i
            middle[outer, j, 8:40, :] += 0.05 * mob[outer, 8:40, :] * outer_in[j]
            return carry

        lax.fori_loop(0, CHUNK, add, 0)
        outer_copy2(k).start()

    def eigen(layer):
        for s in range(4):
            rows = slice(8 + 8 * s, 16 + 8 * s)

            def step(i, totals):
                v = middle[layer, i, rows, :]
                v = v * v
                return tuple(totals[k] + v * eigen_s[i, k] for k in range(3))

            empty = jnp.zeros((8, 512), F32)
            totals = lax.fori_loop(0, 16, step, (empty, empty, empty))
            for k in range(3):
                eig[layer, k, 8 * s : 8 * s + 8, :] = totals[k]

    eigen(other)
    eig_copy = remote(eig.at[other], eig_in.at[c], core_send.at[1], core_recv.at[1], core_peer)
    eig_copy.start()
    eigen(mine)
    to_columns(eig_t, c, (eig[mine, 0], eig[mine, 2], eig[mine, 1], eig[mine, 2]))

    pack(middle, row_out2, col_out2)
    halo2 = [
        remote(row_out2.at[0], row_in2.at[0], halo_send.at[3], halo_recv.at[3], row_up),
        remote(row_out2.at[1], row_in2.at[1], halo_send.at[4], halo_recv.at[4], row_down),
        remote(col_out2, col_in2, halo_send.at[5], halo_recv.at[5], core_peer),
    ]
    for copy in halo2:
        copy.start()

    eig_copy.wait_recv()
    far = [eig_in[1 - c, k] for k in range(3)]
    to_columns(eig_t, 1 - c, (far[0], far[2], far[1], far[2]))

    lane1 = lax.broadcasted_iota(jnp.int32, (128, 128), 1)
    start = jnp.where(
        lane1 < 32, macro_s[0], jnp.where((lane1 >= 64) & (lane1 < 96), macro_s[1], macro_s[2])
    )
    for n1 in range(8):
        strain[n1] = start
    for load in loads[3:]:
        load.wait()

    even16 = (lane16 // 32) % 2 == 0
    lane_all = lax.broadcasted_iota(jnp.int32, (128, 128), 1)
    even = (lane_all // 32) % 2 == 0

    def sweep(it, carry):
        def stage(t, carry):
            rows = pl.ds(pl.multiple_of(t * 16, 16), 16)
            x = []
            for n1 in range(8):
                d = strain[n1, rows, :] - eig_t[n1, rows, :]
                x.append(m1_t[n1, rows, :] * d + m2_t[n1, rows, :] * pltpu.roll(d, 64, 1))
            s04, d04, s26, d26 = x[0] + x[4], x[0] - x[4], x[2] + x[6], x[2] - x[6]
            s15, d15, s37, d37 = x[1] + x[5], x[1] - x[5], x[3] + x[7], x[3] - x[7]
            evens, odds = s04 + s26, s15 + s37
            turned = HALF * (d15 - d37)
            summed = HALF * (d15 + d37)
            values = (
                (evens + odds, evens - odds),
                (d04 + turned, -d26 - summed),
                (s04 - s26, s37 - s15),
                (d04 - turned, d26 - summed),
            )
            rows2 = pl.ds(pl.multiple_of(128 + t * 16, 16), 16)
            for kind, (real, imag) in enumerate(values):
                high[kind, rows, :], low[kind, rows, :] = parts(real)
                high[kind, rows2, :], low[kind, rows2, :] = parts(imag)
            return carry

        lax.fori_loop(0, 8, stage, 0)

        def forward(kk, carry):
            kind = (r // 8 + kk) % 4
            result = dot3(tfh[kind], tfl[kind], high[kind], low[kind])
            send1[it, pl.ds(8 * kind, 8), 0] = result[0:128].reshape(8, 16, 128)
            send1[it, pl.ds(8 * kind, 8), 1] = result[128:256].reshape(8, 16, 128)

            def post(j, carry):
                peer = 8 * kind + (r % 8 + j) % 8

                @pl.when(peer != r)
                def _():
                    remote(
                        send1.at[it, peer], recv1.at[it, r],
                        all_send.at[2 * it], all_recv.at[2 * it], (g, peer, c),
                    ).start()

                return carry

            lax.fori_loop(0, 8, post, 0)
            return carry

        lax.fori_loop(0, 4, forward, 0)
        pltpu.make_async_copy(send1.at[it, r], recv1.at[it, r], all_recv.at[2 * it]).start()
        pltpu.make_async_copy(recv1.at[it], recv1.at[it], all_recv.at[2 * it]).wait()

        for b in range(8):
            x = [(recv1[it, 8 * a + b, 0], recv1[it, 8 * a + b, 1]) for a in range(4)]
            y = four(x, -1)
            for ka in range(4):
                work[ka, b, 0], work[ka, b, 1] = times(y[ka], b * ka, 32, -1)
        for ka in range(4):
            y = eight([(work[ka, b, 0], work[ka, b, 1]) for b in range(8)], -1)
            for kb in range(8):
                k1 = ka + 4 * kb
                cosine, sine = turn[k1, 0:1, :], turn[k1, 1:2, :]
                real, imag = y[kb]
                z = (real * cosine + imag * sine, imag * cosine - real * sine)
                for half in range(2):
                    at = (slice(16 * k1, 16 * k1 + 16), slice(128 * half, 128 * half + 128))
                    lxh[at], lxl[at] = parts(z[half])

        def middle_stage(q, carry):
            rows = pl.ds(pl.multiple_of(q * 128, 128), 128)
            spectrum = dot3(lxh[rows, :], lxl[rows, :], bfh[...], bfl[...])
            group = pl.ds(8 * q, 8)
            g0 = green[0, group].reshape(128, 128)
            g1 = green[1, group].reshape(128, 128)
            g2 = green[2, group].reshape(128, 128)
            pieces = []
            for half in range(2):
                s = spectrum[:, 128 * half : 128 * half + 128]
                z = jnp.where(even, pltpu.roll(s, 64, 1), pltpu.roll(s, 96, 1))
                pieces.append(parts(g0 * s + g1 * z + g2 * pltpu.roll(s, 32, 1)))
            oh = jnp.concatenate([pieces[0][0], pieces[1][0]], axis=1)
            ol = jnp.concatenate([pieces[0][1], pieces[1][1]], axis=1)
            back = dot3(oh, ol, bih[...], bil[...])
            for j in range(8):
                k1 = 8 * q + j
                cosine, sine = turn[k1, 0:1, :], turn[k1, 1:2, :]
                real, imag = back[16 * j : 16 * j + 16, 0:128], back[16 * j : 16 * j + 16, 128:256]
                flat[k1, 0] = real * cosine - imag * sine
                flat[k1, 1] = imag * cosine + real * sine
            return carry

        lax.fori_loop(0, 4, middle_stage, 0)

        for ka in range(4):
            y = eight([(flat[ka + 4 * kb, 0], flat[ka + 4 * kb, 1]) for kb in range(8)], 1)
            for b in range(8):
                work[ka, b, 0], work[ka, b, 1] = times(y[b], b * ka, 32, 1)

        def backward(bb, carry):
            b = (r + bb) % 8
            y = four([(work[ka, b, 0], work[ka, b, 1]) for ka in range(4)], 1)
            for a in range(4):
                send2[it, 8 * a + b, 0], send2[it, 8 * a + b, 1] = y[a]

            def post(j, carry):
                peer = 8 * ((r // 8 + j) % 4) + b

                @pl.when(peer != r)
                def _():
                    remote(
                        send2.at[it, peer], recv2.at[it, r],
                        all_send.at[2 * it + 1], all_recv.at[2 * it + 1], (g, peer, c),
                    ).start()

                return carry

            lax.fori_loop(0, 4, post, 0)
            return carry

        lax.fori_loop(0, 8, backward, 0)
        pltpu.make_async_copy(send2.at[it, r], recv2.at[it, r], all_recv.at[2 * it + 1]).start()
        pltpu.make_async_copy(recv2.at[it], recv2.at[it], all_recv.at[2 * it + 1]).wait()

        def inverse(kind, carry):
            group = pl.ds(8 * kind, 8)
            real = parts(recv2[it, group, 0].reshape(128, 128))
            imag = parts(recv2[it, group, 1].reshape(128, 128))
            high[kind, 0:128], low[kind, 0:128] = real
            high[kind, 128:256], low[kind, 128:256] = imag
            result = dot3(tih[kind], til[kind], high[kind], low[kind])
            flat[pl.ds(8 * kind, 8), 0] = result[0:128].reshape(8, 16, 128)
            flat[pl.ds(8 * kind, 8), 1] = result[128:256].reshape(8, 16, 128)
            return carry

        lax.fori_loop(0, 4, inverse, 0)

        def unstage(t, carry):
            rows = pl.ds(pl.multiple_of(t * 16, 16), 16)
            z0, z4 = flat[t, 0], flat[t, 1]
            a1, b1 = flat[8 + t, 0], flat[8 + t, 1]
            a2, b2 = flat[16 + t, 0], flat[16 + t, 1]
            a3, b3 = flat[24 + t, 0], flat[24 + t, 1]
            zp, zm = z0 + z4, z0 - z4
            sa, db, da, sb = a1 + a3, b3 - b1, a1 - a3, b1 + b3
            p1, p2 = HALF * (da - sb), HALF * (da + sb)
            values = (
                zp + a2 + sa,
                zm - b2 + p1,
                zp - a2 + db,
                zm + b2 - p2,
                zp + a2 - sa,
                zm - b2 - p1,
                zp - a2 - db,
                zm + b2 + p2,
            )
            for n1 in range(8):
                strain[n1, rows, :] -= values[n1]
            return carry

        lax.fori_loop(0, 8, unstage, 0)
        return carry

    lax.fori_loop(0, ITERS, sweep, 0)

    def to_rows(half, layer, target):
        for j in range(4):
            block = strain[4 * half + j].T
            lanes = slice(128 * j, 128 * j + 128)
            target[layer, 0, :, lanes] = block[0:32]
            target[layer, 1, :, lanes] = block[64:96]
            target[layer, 2, :, lanes] = block[32:64]

    to_rows(1 - c, 0, eig_in)
    final_copy = remote(eig_in.at[0], final.at[mine], core_send.at[2], core_recv.at[2], core_peer)
    final_copy.start()
    to_rows(c, mine, final)
    for copy in halo2:
        copy.wait_recv()
    unpack(middle, row_in2)
    remote(eig_in.at[0], final.at[other], core_send.at[2], core_recv.at[2], core_peer).wait_recv()
    strain_ref[...] = final[...]

    def stress_of(layer):
        def at(s):
            rows = slice(8 * s, 8 * s + 8)
            d = [final[layer, k, rows, :] - eig[layer, k, rows, :] for k in range(3)]
            lam, double = lame[layer, 0, rows, :], 2.0 * lame[layer, 1, rows, :]
            return (
                (lam + double) * d[0] + lam * d[1],
                lam * d[0] + (lam + double) * d[1],
                2.0 * (double * d[2]),
            )

        return at

    def to_out(layer, i, s, value):
        out_ref[layer, i, 8 * s : 8 * s + 8, :] = value

    update(middle, col_in2, inner, None, stress_of(inner), to_out)
    for k in range(CHUNKS):
        outer_copy2(k).wait_recv()
    update(middle, col_in2, outer, outer_in2, stress_of(outer), to_out)

    for copy in halo + halo2 + [lame_copy, eig_copy, final_copy]:
        copy.wait_send()
    for k in range(CHUNKS):
        outer_copy(k).wait_send()
        outer_copy2(k).wait_send()
    for it in range(ITERS):
        for sent, sem in ((send1, 2 * it), (send2, 2 * it + 1)):
            whole = sent.at[it, pl.ds(0, ROWS - 1)]
            pltpu.make_async_copy(whole, whole, all_send.at[sem]).wait()


def body(order, grain, phase, mobility, index, stiff, eigen, macro):
    constants = tables()
    any_spec = pl.BlockSpec(memory_space=pl.ANY)
    smem = pl.BlockSpec(memory_space=pltpu.SMEM)
    vmem = pl.BlockSpec(memory_space=pltpu.VMEM)
    big = (2, 16, 48, 512)
    every = (ITERS, ROWS, 2, 16, 128)
    columns = (8, 128, 128)
    return pl.pallas_call(
        kernel,
        out_shape=(
            jax.ShapeDtypeStruct((2, 16, 32, 512), F32),
            jax.ShapeDtypeStruct((2, 3, 32, 512), F32),
        ),
        in_specs=[any_spec] * 12 + [smem] * 5,
        out_specs=(vmem, vmem),
        scratch_shapes=[
            pltpu.VMEM(big, F32),
            pltpu.VMEM(big, F32),
            pltpu.VMEM((2, 48, 512), F32),
            pltpu.VMEM((2, 32, 512), jnp.int32),
            pltpu.VMEM((2, 32, 512), jnp.int32),
        ]
        + [pltpu.VMEM((4, 256, 256), BF16)] * 4
        + [pltpu.VMEM((256, 256), BF16)] * 4
        + [pltpu.VMEM((32, 2, 128), F32)]
        + [
            pltpu.VMEM((2, 34, 1, 512), F32),
            pltpu.VMEM((2, 34, 1, 512), F32),
            pltpu.VMEM((2, 32, 1, 512), F32),
            pltpu.VMEM((2, 32, 1, 512), F32),
            pltpu.VMEM((34, 32, 128), F32),
            pltpu.VMEM((34, 32, 128), F32),
            pltpu.VMEM((32, 32, 128), F32),
            pltpu.VMEM((32, 32, 128), F32),
            pltpu.VMEM((16, 32, 512), F32),
            pltpu.VMEM((16, 32, 512), F32),
            pltpu.VMEM((2, 2, 32, 512), F32),
            pltpu.VMEM((2, 2, 32, 512), F32),
            pltpu.VMEM((2, 3, 32, 512), F32),
            pltpu.VMEM((2, 3, 32, 512), F32),
            pltpu.VMEM((2, 3, 32, 512), F32),
        ]
        + [pltpu.VMEM(columns, F32)] * 4
        + [pltpu.VMEM((3, 32, 16, 128), F32)]
        + [pltpu.VMEM(every, F32)] * 4
        + [pltpu.VMEM((4, 8, 2, 16, 128), F32)]
        + [pltpu.VMEM((4, 256, 128), BF16)] * 2
        + [pltpu.VMEM((32, 2, 16, 128), F32)]
        + [pltpu.VMEM((512, 256), BF16)] * 2
        + [pltpu.SemaphoreType.DMA((n,)) for n in (12, 6, 6, 2 * CHUNKS, 2 * CHUNKS, 3, 3, 2 * ITERS, 2 * ITERS)],
        compiler_params=pltpu.CompilerParams(
            collective_id=0, has_side_effects=True, vmem_limit_bytes=56 * 1024 * 1024
        ),
        name="step",
    )(order, grain, phase, *[jnp.asarray(t) for t in constants], mobility, index, stiff, eigen, macro)


def solution(mesh):
    fields = P("grp", None, "row", "col")
    labels = P("grp", "row", "col")
    return jax.shard_map(
        body,
        mesh=mesh,
        in_specs=(fields, labels, labels, P(), P(), P(), P(), P()),
        out_specs=(fields, fields),
        check_vma=False,
    )
```

time: 585 us -> 124 us (0.21)
  the two profiles are of different devices: /device:TPU:7 before, /device:TPU:1 now
where the time goes in v1:
time: 124 us
  Pallas kernels  116 us (94%)
  local copies, waits for them, and re-layouts  6.68 us (5%)
    pallas_call x1, Pallas kernels, body(): pl.pallas_call(kernel, out_shape=(jax.ShapeDtypeStruct((2, 16, 32, 512),...  116 us
    unnamed x6, local copies, waits for them, and re-layouts  6.68 us

profile of v1, /device:TPU:1, one launch (start us, length us, event | category | flops | bytes accessed | tf_op | source)
XLA Modules:
  0.0 123.5 jit_solution(4823312848077806929)
XLA Ops:
  0.6 1.3 %copy.19.stiff_s = f32[4,2]{1,0:T(4,128)} copy(f32[4,2]{0,1:T(2,128)} %param.22) | data formatting | bytes 64 | tf_op args[5]
  2.0 1.4 %copy.20.eigen_s = f32[16,3]{1,0:T(8,128)} copy(f32[16,3]{0,1:T(4,128)} %param.23) | data formatting | bytes 384 | tf_op args[6]
  3.3 116.2 %step.1 = (f32[2,16,32,512]{3,2,1,0:T(8,128)}, f32[2,3,32,512]{3,2,1,0:T(8,128)}) custom-call(f32[2,16,32,512]{3,2,1,0:T(8,128)} %order_hbm.1, s32[2,32,512]{2,1,0:T(8,128)} %grain_hbm.1, s32[2,32,512]{2,1,0:T(8,128)} %phase_hbm.1, bf16[4,256,256]{2,1,0:T(8,128)(2,1)} %constant.18.clone.tfh_hbm, bf16[4,256,256]{2,1,0:T(8,128)(2,1)} %constant.19.clone.tfl_hbm, ...), custom_call_target="tpu_custom_call" | custom-call | tf_op jit(solution)/shard_map/step/pallas_call | solution.py:644
  119.5 0.0 copy-start
  119.6 3.2 %copy.23 = f32[2,16,32,512]{3,2,1,0:T(8,128)} copy(f32[2,16,32,512]{3,2,1,0:T(8,128)} %get-tuple-element.4) | data formatting | bytes 4194304
  122.8 0.0 copy-done
  122.8 0.7 copy.24
Async XLA Ops:
  119.5 3.2 %copy-start = (f32[2,3,32,512]{3,2,1,0:T(8,128)S(1)}, f32[2,3,32,512]{3,2,1,0:T(8,128)}, u32[]{:S(2)}) copy-start(f32[2,3,32,512]{3,2,1,0:T(8,128)} %get-tuple-element.5) | copy-start | bytes 1179652

commit v2 on v1

--- a/solution.py
+++ b/solution.py
@@ -18,6 +18,7 @@
 BF16 = jnp.bfloat16
 CHUNK = 4
 CHUNKS = 16 // CHUNK
+UNROLL = 4
 
 
 def split_table(values):
@@ -116,7 +117,7 @@
     out_ref, strain_ref,
     first, middle, mob, grain, phase, tfh, tfl, tih, til, bfh, bfl, bih, bil, turn,
     row_out, row_in, row_out2, row_in2, col_out, col_in, col_out2, col_in2,
-    outer_in, outer_in2, lame, lame_in, eig, eig_in, final,
+    base, outer_in, outer_in2, lame, lame_in, eig, eig_in, final,
     strain, eig_t, m1_t, m2_t, green, send1, recv1, send2, recv2, work, high, low, flat, lxh, lxl,
     load_sem, halo_send, halo_recv, outer_send, outer_recv, core_send, core_recv, all_send, all_recv,
 ):
@@ -175,8 +176,8 @@
             chosen = index_s[k]
             hit = labels2 == k
             return (
-                jnp.where(hit, stiff_s[chosen, 0], values[0]),
-                jnp.where(hit, stiff_s[chosen, 1], values[1]),
+                jnp.where(hit, stiff_s[0, chosen], values[0]),
+                jnp.where(hit, stiff_s[1, chosen], values[1]),
             )
 
         empty = jnp.zeros((32, 512), F32)
@@ -308,7 +309,7 @@
         mob[layer, 40:41, :] = row_in[0, 32 + layer]
         mob[layer, 7:8, :] = row_in[1, 32 + layer]
 
-    def update(source, cols, layer, beyond, stress, write):
+    def update(source, cols, layer, write):
         for s in range(4):
             r0, r1 = 8 + 8 * s, 8 * s
             m = mob[layer, r0 : r0 + 8, :]
@@ -317,48 +318,51 @@
             w_down = 0.05 * (m + mob[layer, r0 + 1 : r0 + 9, :])
             w_left = 0.05 * (m + pltpu.roll(edge, 1, 1)[:, 128:])
             w_right = 0.05 * (m + pltpu.roll(edge, 639, 1)[:, 128:])
-
-            def square(i, total):
+            total = jnp.zeros((8, 512), F32)
+            for i in range(16):
                 v = source[layer, i, r0 : r0 + 8, :]
-                return total + v * v
-
-            total = lax.fori_loop(0, 16, square, jnp.zeros((8, 512), F32))
+                total = total + v * v
             c0 = 1.0 - (w_up + w_down + w_left + w_right) - 0.3 * m * total
             c1 = 0.2 * m
             m05 = 0.05 * m
-            push = None if stress is None else [c1 * p for p in stress(s)]
-
-            def step(i, carry):
-                v = source[layer, i, r0 : r0 + 8, :]
-                e = jnp.concatenate([cols[layer * 16 + i, r1 : r1 + 8, :], v], axis=1)
-                left = pltpu.roll(e, 1, 1)[:, 128:]
-                right = pltpu.roll(e, 639, 1)[:, 128:]
-                near = source[1 - layer, i, r0 : r0 + 8, :]
-                if beyond is not None:
-                    near = near + beyond[i, r1 : r1 + 8, :]
-                factor = c0 + c1 * v * v
-                if push is not None:
-                    factor = factor + (
-                        push[0] * eigen_s[i, 0] + push[1] * eigen_s[i, 1] + push[2] * eigen_s[i, 2]
+
+            def step(n, carry):
+                for i4 in range(UNROLL):
+                    i = n * UNROLL + i4
+                    v = source[layer, i, r0 : r0 + 8, :]
+                    e = jnp.concatenate([cols[layer * 16 + i, r1 : r1 + 8, :], v], axis=1)
+                    write(
+                        layer,
+                        i,
+                        s,
+                        v * (c0 + c1 * v * v)
+                        + w_up * source[layer, i, r0 - 1 : r0 + 7, :]
+                        + w_down * source[layer, i, r0 + 1 : r0 + 9, :]
+                        + w_left * pltpu.roll(e, 1, 1)[:, 128:]
+                        + w_right * pltpu.roll(e, 639, 1)[:, 128:]
+                        + m05 * source[1 - layer, i, r0 : r0 + 8, :],
                     )
-                value = (
-                    v * factor
-                    + w_up * source[layer, i, r0 - 1 : r0 + 7, :]
-                    + w_down * source[layer, i, r0 + 1 : r0 + 9, :]
-                    + w_left * left
-                    + w_right * right
-                    + m05 * near
-                )
-                write(layer, i, s, value)
                 return carry
 
-            lax.fori_loop(0, 16, step, 0)
+            lax.fori_loop(0, 16 // UNROLL, step, 0)
 
     def to_middle(layer, i, s, value):
         middle[layer, i, 8 + 8 * s : 16 + 8 * s, :] = value
 
-    update(first, col_in, outer, None, None, to_middle)
-    update(first, col_in, inner, None, None, to_middle)
+    def to_base(layer, i, s, value):
+        base[layer, i, 8 * s : 8 * s + 8, :] = value
+
+    update(first, col_in, inner, to_middle)
+    for s in range(4):
+        totals = [jnp.zeros((8, 512), F32)] * 3
+        for i in range(16):
+            v = middle[inner, i, 8 + 8 * s : 16 + 8 * s, :]
+            v = v * v
+            totals = [totals[k] + v * eigen_s[k, i] for k in range(3)]
+        for k in range(3):
+            eig[inner, k, 8 * s : 8 * s + 8, :] = totals[k]
+            eig[outer, k, 8 * s : 8 * s + 8, :] = jnp.zeros((8, 512), F32)
+    update(first, col_in, outer, to_middle)
 
     lame_copy.wait_recv()
     stiff_columns(1 - c, lame_in[1 - c, 0], lame_in[1 - c, 1])
@@ -366,42 +370,30 @@
     for k in range(CHUNKS):
         outer_copy(k).wait_recv()
 
-        def add(i, carry):
-            j = k * CHUNK + i
-            middle[outer, j, 8:40, :] += 0.05 * mob[outer, 8:40, :] * outer_in[j]
-            return carry
-
-        lax.fori_loop(0, CHUNK, add, 0)
-        outer_copy2(k).start()
-
-    def eigen(layer):
-        for s in range(4):
-            rows = slice(8 + 8 * s, 16 + 8 * s)
-
-            def step(i, totals):
-                v = middle[layer, i, rows, :]
+        def add(s, carry):
+            at, at2 = pl.ds(pl.multiple_of(8 + 8 * s, 8), 8), pl.ds(pl.multiple_of(8 * s, 8), 8)
+            m05 = 0.05 * mob[outer, at, :]
+            totals = [eig[outer, n, at2, :] for n in range(3)]
+            for i in range(CHUNK):
+                j = k * CHUNK + i
+                v = middle[outer, j, at, :] + m05 * outer_in[j, at2, :]
+                middle[outer, j, at, :] = v
                 v = v * v
-                return tuple(totals[k] + v * eigen_s[i, k] for k in range(3))
-
-            empty = jnp.zeros((8, 512), F32)
-            totals = lax.fori_loop(0, 16, step, (empty, empty, empty))
-            for k in range(3):
-                eig[layer, k, 8 * s : 8 * s + 8, :] = totals[k]
-
-    eigen(other)
+                totals = [totals[n] + v * eigen_s[n, j] for n in range(3)]
+            for n in range(3):
+                eig[outer, n, at2, :] = totals[n]
+            return carry
+
+        lax.fori_loop(0, 4, add, 0)
+
     eig_copy = remote(eig.at[other], eig_in.at[c], core_send.at[1], core_recv.at[1], core_peer)
     eig_copy.start()
-    eigen(mine)
     to_columns(eig_t, c, (eig[mine, 0], eig[mine, 2], eig[mine, 1], eig[mine, 2]))
-
-    pack(middle, row_out2, col_out2)
     halo2 = [
         remote(row_out2.at[0], row_in2.at[0], halo_send.at[3], halo_recv.at[3], row_up),
         remote(row_out2.at[1], row_in2.at[1], halo_send.at[4], halo_recv.at[4], row_down),
         remote(col_out2, col_in2, halo_send.at[5], halo_recv.at[5], core_peer),
     ]
-    for copy in halo2:
-        copy.start()
 
     eig_copy.wait_recv()
     far = [eig_in[1 - c, k] for k in range(3)]
@@ -469,6 +461,14 @@
 
         lax.fori_loop(0, 4, forward, 0)
         pltpu.make_async_copy(send1.at[it, r], recv1.at[it, r], all_recv.at[2 * it]).start()
+        outer_copy2(2 * it).start()
+
+        @pl.when(it == 0)
+        def _():
+            pack(middle, row_out2, col_out2)
+            for copy in halo2:
+                copy.start()
+
         pltpu.make_async_copy(recv1.at[it], recv1.at[it], all_recv.at[2 * it]).wait()
 
         for b in range(8):
@@ -540,6 +540,15 @@
 
         lax.fori_loop(0, 8, backward, 0)
         pltpu.make_async_copy(send2.at[it, r], recv2.at[it, r], all_recv.at[2 * it + 1]).start()
+        outer_copy2(2 * it + 1).start()
+
+        @pl.when(it == 0)
+        def _():
+            for copy in halo2:
+                copy.wait_recv()
+            unpack(middle, row_in2)
+
+        update(middle, col_in2, it, to_base)
         pltpu.make_async_copy(recv2.at[it], recv2.at[it], all_recv.at[2 * it + 1]).wait()
 
         def inverse(kind, carry):
@@ -595,32 +604,37 @@
     final_copy = remote(eig_in.at[0], final.at[mine], core_send.at[2], core_recv.at[2], core_peer)
     final_copy.start()
     to_rows(c, mine, final)
-    for copy in halo2:
-        copy.wait_recv()
-    unpack(middle, row_in2)
     remote(eig_in.at[0], final.at[other], core_send.at[2], core_recv.at[2], core_peer).wait_recv()
     strain_ref[...] = final[...]
 
-    def stress_of(layer):
-        def at(s):
-            rows = slice(8 * s, 8 * s + 8)
+    def finish(layer, beyond):
+        def at(s, carry):
+            rows = pl.ds(pl.multiple_of(8 * s, 8), 8)
             d = [final[layer, k, rows, :] - eig[layer, k, rows, :] for k in range(3)]
             lam, double = lame[layer, 0, rows, :], 2.0 * lame[layer, 1, rows, :]
-            return (
-                (lam + double) * d[0] + lam * d[1],
-                lam * d[0] + (lam + double) * d[1],
-                2.0 * (double * d[2]),
+            m = mob[layer, pl.ds(pl.multiple_of(8 + 8 * s, 8), 8), :]
+            m05, c1 = 0.05 * m, 0.2 * m
+            push = (
+                c1 * ((lam + double) * d[0] + lam * d[1]),
+                c1 * (lam * d[0] + (lam + double) * d[1]),
+                c1 * (2.0 * (double * d[2])),
             )
-
-        return at
-
-    def to_out(layer, i, s, value):
-        out_ref[layer, i, 8 * s : 8 * s + 8, :] = value
-
-    update(middle, col_in2, inner, None, stress_of(inner), to_out)
+            for i in range(16):
+                v = middle[layer, i, pl.ds(pl.multiple_of(8 + 8 * s, 8), 8), :]
+                value = base[layer, i, rows, :] + v * (
+                    push[0] * eigen_s[0, i] + push[1] * eigen_s[1, i] + push[2] * eigen_s[2, i]
+                )
+                if beyond:
+                    value = value + m05 * outer_in2[i, rows, :]
+                out_ref[layer, i, rows, :] = value
+            return carry
+
+        lax.fori_loop(0, 4, at, 0)
+
+    finish(inner, False)
     for k in range(CHUNKS):
         outer_copy2(k).wait_recv()
-    update(middle, col_in2, outer, outer_in2, stress_of(outer), to_out)
+    finish(outer, True)
 
     for copy in halo + halo2 + [lame_copy, eig_copy, final_copy]:
         copy.wait_send()
@@ -668,6 +682,7 @@
             pltpu.VMEM((34, 32, 128), F32),
             pltpu.VMEM((32, 32, 128), F32),
             pltpu.VMEM((32, 32, 128), F32),
+            pltpu.VMEM((2, 16, 32, 512), F32),
             pltpu.VMEM((16, 32, 512), F32),
             pltpu.VMEM((16, 32, 512), F32),
             pltpu.VMEM((2, 2, 32, 512), F32),
@@ -688,7 +703,7 @@
             collective_id=0, has_side_effects=True, vmem_limit_bytes=56 * 1024 * 1024
         ),
         name="step",
-    )(order, grain, phase, *[jnp.asarray(t) for t in constants], mobility, index, stiff, eigen, macro)
+    )(order, grain, phase, *[jnp.asarray(t) for t in constants], mobility, index, stiff.T, eigen.T, macro)
 
 
 def solution(mesh):

time: 124 us -> 97.6 us (0.79)
  Pallas kernels: 116 us -> 92.8 us
  local copies, waits for them, and re-layouts: 6.68 us -> 3.99 us
    pallas_call x1, Pallas kernels: 116 us -> 92.8 us  [body(): pl.pallas_call(kernel, out_shape=(jax.ShapeDtypeStruct((2, 16, 32, 512),...]
    unnamed x6 -> x4, local copies, waits for them, and re-layouts: 6.68 us -> 3.99 us
where the time goes in v2:
time: 97.6 us; the launch traced here: 97.5 us
  Pallas kernels  92.8 us (95%)
  local copies, waits for them, and re-layouts  3.99 us (4%)
    pallas_call x1, Pallas kernels, body(): pl.pallas_call(kernel, out_shape=(jax.ShapeDtypeStruct((2, 16, 32, 512),...  92.8 us
    unnamed x4, local copies, waits for them, and re-layouts  3.99 us

profile of v2, /device:TPU:1, one launch (start us, length us, event | category | flops | bytes accessed | tf_op | source)
XLA Modules:
  0.0 97.5 jit_solution(2364347345550997709)
XLA Ops:
  0.6 92.8 %step.1 = (f32[2,16,32,512]{3,2,1,0:T(8,128)}, f32[2,3,32,512]{3,2,1,0:T(8,128)}) custom-call(f32[2,16,32,512]{3,2,1,0:T(8,128)} %order_hbm.1, s32[2,32,512]{2,1,0:T(8,128)} %grain_hbm.1, s32[2,32,512]{2,1,0:T(8,128)} %phase_hbm.1, bf16[4,256,256]{2,1,0:T(8,128)(2,1)} %constant.18.clone.tfh_hbm, bf16[4,256,256]{2,1,0:T(8,128)(2,1)} %constant.19.clone.tfl_hbm, ...), custom_call_target="tpu_custom_call" | custom-call | tf_op jit(solution)/shard_map/step/pallas_call | solution.py:658
  93.5 0.0 copy-start
  93.5 3.2 %copy.21 = f32[2,16,32,512]{3,2,1,0:T(8,128)} copy(f32[2,16,32,512]{3,2,1,0:T(8,128)} %get-tuple-element.4) | data formatting | bytes 4194304
  96.7 0.0 copy-done
  96.7 0.7 copy.22
Async XLA Ops:
  93.5 3.2 %copy-start = (f32[2,3,32,512]{3,2,1,0:T(8,128)S(1)}, f32[2,3,32,512]{3,2,1,0:T(8,128)}, u32[]{:S(2)}) copy-start(f32[2,3,32,512]{3,2,1,0:T(8,128)} %get-tuple-element.5) | copy-start | bytes 1179652

commit v3 on v2

--- a/solution.py
+++ b/solution.py
@@ -19,6 +19,7 @@
 CHUNK = 4
 CHUNKS = 16 // CHUNK
 UNROLL = 4
+EARLY = 1
 
 
 def split_table(values):
@@ -50,9 +51,13 @@
         inverse[kind] = 2.0 * scale * np.block([[cosine.T, -sine.T], [sine.T, cosine.T]])
     small = np.arange(32, dtype=np.float64)
     angle = 2.0 * np.pi * np.outer(small, small) / 32.0
-    cosine, sine = np.kron(np.eye(4), np.cos(angle)), np.kron(np.eye(4), np.sin(angle))
+    slots = np.eye(4)
+    slots[3, 3] = 0.0
+    cosine, sine = np.kron(slots, np.cos(angle)), np.kron(slots, np.sin(angle))
+    rows_inverse = np.block([[cosine, sine], [-sine, cosine]])
+    slots[1, 3] = 1.0
+    cosine, sine = np.kron(slots, np.cos(angle)), np.kron(slots, np.sin(angle))
     rows_forward = np.block([[cosine, -sine], [sine, cosine]])
-    rows_inverse = np.block([[cosine, sine], [-sine, cosine]])
     angle = 2.0 * np.pi * np.outer(small, np.tile(small, 4)) / 1024.0
     turn = np.stack([np.cos(angle), np.sin(angle)], axis=1).astype(np.float32)
     return (
@@ -114,12 +119,12 @@
 def kernel(
     order_hbm, grain_hbm, phase_hbm, tfh_hbm, tfl_hbm, tih_hbm, til_hbm, bfh_hbm, bfl_hbm, bih_hbm,
     bil_hbm, turn_hbm, mob_s, index_s, stiff_s, eigen_s, macro_s,
-    out_ref, strain_ref,
-    first, middle, mob, grain, phase, tfh, tfl, tih, til, bfh, bfl, bih, bil, turn,
+    middle, base, outer_in2, final, eig, lame, mob,
+    first, grain, phase, tfh, tfl, tih, til, bfh, bfl, bih, bil, turn,
     row_out, row_in, row_out2, row_in2, col_out, col_in, col_out2, col_in2,
-    base, outer_in, outer_in2, lame, lame_in, eig, eig_in, final,
-    strain, eig_t, m1_t, m2_t, green, send1, recv1, send2, recv2, work, high, low, flat, lxh, lxl,
-    load_sem, halo_send, halo_recv, outer_send, outer_recv, core_send, core_recv, all_send, all_recv,
+    outer_in, lame_in, eig_in,
+    strain, eig_t, m1_t, m2_t, green, send1, recv1, send2, recv2, work, both, flat, lxh, lxl,
+    load_sem, halo_send, halo_recv, outer_send, outer_recv, core_send, core_recv, all_send, all_recv, meet_sem,
 ):
     g, r, c = lax.axis_index("grp"), lax.axis_index("row"), lax.axis_index("col")
     inner, outer = g, 1 - g
@@ -150,16 +155,16 @@
         load.start()
 
     barrier = pltpu.get_barrier_semaphore()
-    pl.semaphore_signal(barrier, inc=1, device_id=grp_peer, device_id_type=MESH)
-    pl.semaphore_signal(barrier, inc=1, device_id=core_peer, device_id_type=MESH)
-
-    def greet(step, carry):
-        pl.semaphore_signal(
-            barrier, inc=1, device_id=(g, (r + step) % ROWS, c), device_id_type=MESH
-        )
-        return carry
-
-    lax.fori_loop(1, ROWS, greet, 0)
+    beyond = jnp.where(r % 2 == 1, row_down[1], row_up[1])
+    near = [(g, jnp.bitwise_xor(r, 1 << k), c) for k in range(5)]
+    for peer in [grp_peer, core_peer, (g, beyond, c)] + near:
+        pl.semaphore_signal(barrier, inc=1, device_id=peer, device_id_type=MESH)
+
+    def meet(k):
+        if k > 0:
+            pl.semaphore_wait(meet_sem.at[k - 1], 1)
+        if k < 5:
+            pl.semaphore_signal(meet_sem.at[k], inc=1, device_id=near[k], device_id_type=MESH)
 
     loads[0].wait()
     loads[1].wait()
@@ -217,7 +222,8 @@
         row_out[1, 32 + layer] = mob[layer, 39:40, :]
         col_out[32 + layer] = jnp.where(lane < 64, mob[layer, 8:40, 0:128], mob[layer, 8:40, 384:512])
 
-    pl.semaphore_wait(barrier, ROWS + 1)
+    pl.semaphore_wait(barrier, 8)
+    meet(0)
 
     halo = [
         remote(row_out.at[0], row_in.at[0], halo_send.at[0], halo_recv.at[0], row_up),
@@ -287,6 +293,7 @@
         return carry
 
     lax.fori_loop(0, 32, green_step, 0)
+    meet(1)
 
     def to_columns(target, half, slots):
         for j in range(4):
@@ -296,14 +303,15 @@
     def stiff_columns(half, lam, shear):
         double = 2.0 * shear
         straight = lam + double
-        to_columns(m1_t, half, (straight, double, straight, double))
         empty = jnp.zeros_like(lam)
+        to_columns(m1_t, half, (straight, double, straight, empty))
         to_columns(m2_t, half, (lam, empty, lam, empty))
 
     stiff_columns(c, lame[mine, 0], lame[mine, 1])
 
     for copy in halo:
         copy.wait_recv()
+    meet(2)
     unpack(first, row_in)
     for layer in range(2):
         mob[layer, 40:41, :] = row_in[0, 32 + layer]
@@ -353,6 +361,7 @@
         base[layer, i, 8 * s : 8 * s + 8, :] = value
 
     update(first, col_in, inner, to_middle)
+    meet(3)
     for s in range(4):
         totals = [jnp.zeros((8, 512), F32)] * 3
         for i in range(16):
@@ -363,12 +372,15 @@
             eig[inner, k, 8 * s : 8 * s + 8, :] = totals[k]
             eig[outer, k, 8 * s : 8 * s + 8, :] = jnp.zeros((8, 512), F32)
     update(first, col_in, outer, to_middle)
+    meet(4)
 
     lame_copy.wait_recv()
     stiff_columns(1 - c, lame_in[1 - c, 0], lame_in[1 - c, 1])
 
     for k in range(CHUNKS):
         outer_copy(k).wait_recv()
+        if k == 2:
+            meet(5)
 
         def add(s, carry):
             at, at2 = pl.ds(pl.multiple_of(8 + 8 * s, 8), 8), pl.ds(pl.multiple_of(8 * s, 8), 8)
@@ -385,6 +397,8 @@
             return carry
 
         lax.fori_loop(0, 4, add, 0)
+        if k < EARLY:
+            outer_copy2(k).start()
 
     eig_copy = remote(eig.at[other], eig_in.at[c], core_send.at[1], core_recv.at[1], core_peer)
     eig_copy.start()
@@ -411,6 +425,19 @@
     even16 = (lane16 // 32) % 2 == 0
     lane_all = lax.broadcasted_iota(jnp.int32, (128, 128), 1)
     even = (lane_all // 32) % 2 == 0
+
+    def product(table_high, table_low, kind):
+        wide = dot(table_high[kind], both[kind])
+        return wide[:, 0:128] + wide[:, 128:256] + dot(table_low[kind], both[kind, :, 0:128])
+
+    def pack3(a):
+        slot = lax.broadcasted_iota(jnp.int32, a[0].shape, 1) // 32
+        return [jnp.where(slot == 3, pltpu.roll(a[3], 96 - 32 * k, 1), a[k]) for k in range(3)]
+
+    def unpack3(p):
+        slot = lax.broadcasted_iota(jnp.int32, p[0].shape, 1) // 32
+        x, y, z = (pltpu.roll(p[k], 32 + 32 * k, 1) for k in range(3))
+        return list(p) + [jnp.where(slot == 0, x, jnp.where(slot == 1, y, z))]
 
     def sweep(it, carry):
         def stage(t, carry):
@@ -432,17 +459,18 @@
             )
             rows2 = pl.ds(pl.multiple_of(128 + t * 16, 16), 16)
             for kind, (real, imag) in enumerate(values):
-                high[kind, rows, :], low[kind, rows, :] = parts(real)
-                high[kind, rows2, :], low[kind, rows2, :] = parts(imag)
+                both[kind, rows, 0:128], both[kind, rows, 128:256] = parts(real)
+                both[kind, rows2, 0:128], both[kind, rows2, 128:256] = parts(imag)
             return carry
 
         lax.fori_loop(0, 8, stage, 0)
 
         def forward(kk, carry):
             kind = (r // 8 + kk) % 4
-            result = dot3(tfh[kind], tfl[kind], high[kind], low[kind])
-            send1[it, pl.ds(8 * kind, 8), 0] = result[0:128].reshape(8, 16, 128)
-            send1[it, pl.ds(8 * kind, 8), 1] = result[128:256].reshape(8, 16, 128)
+            result = product(tfh, tfl, kind).reshape(2, 8, 2, 8, 128)
+            packed = pack3([result[n // 2, :, n % 2].reshape(64, 128) for n in range(4)])
+            for n in range(3):
+                send1[it, pl.ds(8 * kind, 8), n] = packed[n].reshape(8, 8, 128)
 
             def post(j, carry):
                 peer = 8 * kind + (r % 8 + j) % 8
@@ -461,7 +489,7 @@
 
         lax.fori_loop(0, 4, forward, 0)
         pltpu.make_async_copy(send1.at[it, r], recv1.at[it, r], all_recv.at[2 * it]).start()
-        outer_copy2(2 * it).start()
+        outer_copy2(2 * it + 1).start()
 
         @pl.when(it == 0)
         def _():
@@ -472,7 +500,10 @@
         pltpu.make_async_copy(recv1.at[it], recv1.at[it], all_recv.at[2 * it]).wait()
 
         for b in range(8):
-            x = [(recv1[it, 8 * a + b, 0], recv1[it, 8 * a + b, 1]) for a in range(4)]
+            x = []
+            for a in range(4):
+                v = unpack3([recv1[it, 8 * a + b, n] for n in range(3)])
+                x.append((jnp.concatenate(v[0:2], axis=0), jnp.concatenate(v[2:4], axis=0)))
             y = four(x, -1)
             for ka in range(4):
                 work[ka, b, 0], work[ka, b, 1] = times(y[ka], b * ka, 32, -1)
@@ -521,7 +552,9 @@
             b = (r + bb) % 8
             y = four([(work[ka, b, 0], work[ka, b, 1]) for ka in range(4)], 1)
             for a in range(4):
-                send2[it, 8 * a + b, 0], send2[it, 8 * a + b, 1] = y[a]
+                packed = pack3([y[a][n // 2][8 * (n % 2) : 8 * (n % 2) + 8] for n in range(4)])
+                for n in range(3):
+                    send2[it, 8 * a + b, n] = packed[n]
 
             def post(j, carry):
                 peer = 8 * ((r // 8 + j) % 4) + b
@@ -540,10 +573,10 @@
 
         lax.fori_loop(0, 8, backward, 0)
         pltpu.make_async_copy(send2.at[it, r], recv2.at[it, r], all_recv.at[2 * it + 1]).start()
-        outer_copy2(2 * it + 1).start()
 
         @pl.when(it == 0)
         def _():
+            outer_copy2(2).start()
             for copy in halo2:
                 copy.wait_recv()
             unpack(middle, row_in2)
@@ -553,11 +586,13 @@
 
         def inverse(kind, carry):
             group = pl.ds(8 * kind, 8)
-            real = parts(recv2[it, group, 0].reshape(128, 128))
-            imag = parts(recv2[it, group, 1].reshape(128, 128))
-            high[kind, 0:128], low[kind, 0:128] = real
-            high[kind, 128:256], low[kind, 128:256] = imag
-            result = dot3(tih[kind], til[kind], high[kind], low[kind])
+            v = unpack3([recv2[it, group, n].reshape(64, 128) for n in range(3)])
+            for half in range(2):
+                at = slice(128 * half, 128 * half + 128)
+                pair = [v[2 * half + n].reshape(8, 1, 8, 128) for n in range(2)]
+                value = parts(jnp.concatenate(pair, axis=1).reshape(128, 128))
+                both[kind, at, 0:128], both[kind, at, 128:256] = value
+            result = product(tih, til, kind)
             flat[pl.ds(8 * kind, 8), 0] = result[0:128].reshape(8, 16, 128)
             flat[pl.ds(8 * kind, 8), 1] = result[128:256].reshape(8, 16, 128)
             return carry
@@ -605,37 +640,8 @@
     final_copy.start()
     to_rows(c, mine, final)
     remote(eig_in.at[0], final.at[other], core_send.at[2], core_recv.at[2], core_peer).wait_recv()
-    strain_ref[...] = final[...]
-
-    def finish(layer, beyond):
-        def at(s, carry):
-            rows = pl.ds(pl.multiple_of(8 * s, 8), 8)
-            d = [final[layer, k, rows, :] - eig[layer, k, rows, :] for k in range(3)]
-            lam, double = lame[layer, 0, rows, :], 2.0 * lame[layer, 1, rows, :]
-            m = mob[layer, pl.ds(pl.multiple_of(8 + 8 * s, 8), 8), :]
-            m05, c1 = 0.05 * m, 0.2 * m
-            push = (
-                c1 * ((lam + double) * d[0] + lam * d[1]),
-                c1 * (lam * d[0] + (lam + double) * d[1]),
-                c1 * (2.0 * (double * d[2])),
-            )
-            for i in range(16):
-                v = middle[layer, i, pl.ds(pl.multiple_of(8 + 8 * s, 8), 8), :]
-                value = base[layer, i, rows, :] + v * (
-                    push[0] * eigen_s[0, i] + push[1] * eigen_s[1, i] + push[2] * eigen_s[2, i]
-                )
-                if beyond:
-                    value = value + m05 * outer_in2[i, rows, :]
-                out_ref[layer, i, rows, :] = value
-            return carry
-
-        lax.fori_loop(0, 4, at, 0)
-
-    finish(inner, False)
     for k in range(CHUNKS):
         outer_copy2(k).wait_recv()
-    finish(outer, True)
-
     for copy in halo + halo2 + [lame_copy, eig_copy, final_copy]:
         copy.wait_send()
     for k in range(CHUNKS):
@@ -647,26 +653,70 @@
             pltpu.make_async_copy(whole, whole, all_send.at[sem]).wait()
 
 
+def finish(
+    middle, base, outer_in2, final, eig, lame, mob, eigen_s, out_hbm, strain_hbm, out, sem
+):
+    g = lax.axis_index("grp")
+    strain_copy = pltpu.make_async_copy(final, strain_hbm, sem.at[8])
+    strain_copy.start()
+    for place in range(2):
+        layer = g if place == 0 else 1 - g
+
+        def at(s, carry):
+            rows = pl.ds(pl.multiple_of(8 * s, 8), 8)
+            rows2 = pl.ds(pl.multiple_of(8 + 8 * s, 8), 8)
+            d = [final[layer, k, rows, :] - eig[layer, k, rows, :] for k in range(3)]
+            lam, double = lame[layer, 0, rows, :], 2.0 * lame[layer, 1, rows, :]
+            m = mob[layer, rows2, :]
+            m05, c1 = 0.05 * m, 0.2 * m
+            push = (
+                c1 * ((lam + double) * d[0] + lam * d[1]),
+                c1 * (lam * d[0] + (lam + double) * d[1]),
+                c1 * (2.0 * (double * d[2])),
+            )
+            for i in range(16):
+                v = middle[layer, i, rows2, :]
+                value = base[layer, i, rows, :] + v * (
+                    push[0] * eigen_s[0, i] + push[1] * eigen_s[1, i] + push[2] * eigen_s[2, i]
+                )
+                if place == 1:
+                    value = value + m05 * outer_in2[i, rows, :]
+                out[layer, i, rows, :] = value
+            pltpu.make_async_copy(
+                out.at[layer, :, rows, :], out_hbm.at[layer, :, rows, :], sem.at[4 * place + s]
+            ).start()
+            return carry
+
+        lax.fori_loop(0, 4, at, 0)
+    for place in range(2):
+        layer = g if place == 0 else 1 - g
+        for s in range(4):
+            rows = pl.ds(8 * s, 8)
+            pltpu.make_async_copy(
+                out.at[layer, :, rows, :], out_hbm.at[layer, :, rows, :], sem.at[4 * place + s]
+            ).wait()
+    strain_copy.wait()
+
+
 def body(order, grain, phase, mobility, index, stiff, eigen, macro):
     constants = tables()
     any_spec = pl.BlockSpec(memory_space=pl.ANY)
     smem = pl.BlockSpec(memory_space=pltpu.SMEM)
     vmem = pl.BlockSpec(memory_space=pltpu.VMEM)
     big = (2, 16, 48, 512)
-    every = (ITERS, ROWS, 2, 16, 128)
+    every = (ITERS, ROWS, 3, 8, 128)
     columns = (8, 128, 128)
-    return pl.pallas_call(
+    kept = (
+        big, (2, 16, 32, 512), (16, 32, 512), (2, 3, 32, 512), (2, 3, 32, 512), (2, 2, 32, 512),
+        (2, 48, 512),
+    )
+    values = pl.pallas_call(
         kernel,
-        out_shape=(
-            jax.ShapeDtypeStruct((2, 16, 32, 512), F32),
-            jax.ShapeDtypeStruct((2, 3, 32, 512), F32),
-        ),
+        out_shape=tuple(pltpu.VMEM(shape, F32) for shape in kept),
         in_specs=[any_spec] * 12 + [smem] * 5,
-        out_specs=(vmem, vmem),
+        out_specs=(vmem,) * len(kept),
         scratch_shapes=[
             pltpu.VMEM(big, F32),
-            pltpu.VMEM(big, F32),
-            pltpu.VMEM((2, 48, 512), F32),
             pltpu.VMEM((2, 32, 512), jnp.int32),
             pltpu.VMEM((2, 32, 512), jnp.int32),
         ]
@@ -682,28 +732,39 @@
             pltpu.VMEM((34, 32, 128), F32),
             pltpu.VMEM((32, 32, 128), F32),
             pltpu.VMEM((32, 32, 128), F32),
-            pltpu.VMEM((2, 16, 32, 512), F32),
-            pltpu.VMEM((16, 32, 512), F32),
             pltpu.VMEM((16, 32, 512), F32),
             pltpu.VMEM((2, 2, 32, 512), F32),
-            pltpu.VMEM((2, 2, 32, 512), F32),
-            pltpu.VMEM((2, 3, 32, 512), F32),
-            pltpu.VMEM((2, 3, 32, 512), F32),
             pltpu.VMEM((2, 3, 32, 512), F32),
         ]
         + [pltpu.VMEM(columns, F32)] * 4
         + [pltpu.VMEM((3, 32, 16, 128), F32)]
         + [pltpu.VMEM(every, F32)] * 4
         + [pltpu.VMEM((4, 8, 2, 16, 128), F32)]
-        + [pltpu.VMEM((4, 256, 128), BF16)] * 2
+        + [pltpu.VMEM((4, 256, 256), BF16)]
         + [pltpu.VMEM((32, 2, 16, 128), F32)]
         + [pltpu.VMEM((512, 256), BF16)] * 2
-        + [pltpu.SemaphoreType.DMA((n,)) for n in (12, 6, 6, 2 * CHUNKS, 2 * CHUNKS, 3, 3, 2 * ITERS, 2 * ITERS)],
+        + [
+            pltpu.SemaphoreType.DMA((n,))
+            for n in (12, 6, 6, 2 * CHUNKS, 2 * CHUNKS, 3, 3, 2 * ITERS, 2 * ITERS)
+        ]
+        + [pltpu.SemaphoreType.REGULAR((5,))],
         compiler_params=pltpu.CompilerParams(
-            collective_id=0, has_side_effects=True, vmem_limit_bytes=56 * 1024 * 1024
+            collective_id=0, has_side_effects=True, vmem_limit_bytes=48 * 1024 * 1024
         ),
         name="step",
     )(order, grain, phase, *[jnp.asarray(t) for t in constants], mobility, index, stiff.T, eigen.T, macro)
+    return pl.pallas_call(
+        finish,
+        out_shape=(
+            jax.ShapeDtypeStruct((2, 16, 32, 512), F32),
+            jax.ShapeDtypeStruct((2, 3, 32, 512), F32),
+        ),
+        in_specs=[vmem] * len(kept) + [smem],
+        out_specs=(any_spec, any_spec),
+        scratch_shapes=[pltpu.VMEM((2, 16, 32, 512), F32), pltpu.SemaphoreType.DMA((9,))],
+        compiler_params=pltpu.CompilerParams(vmem_limit_bytes=6 * 1024 * 1024),
+        name="finish",
+    )(*values, eigen.T)
 
 
 def solution(mesh):

time: 97.6 us -> 88.6 us (0.908)
  Pallas kernels: 92.8 us -> 87.8 us
  local copies, waits for them, and re-layouts: 3.99 us -> 0.01 us
    pallas_call x1 -> x2, Pallas kernels: 92.8 us -> 87.8 us  [the longest x1 85.7 us: body(): pl.pallas_call(kernel, out_shape=tuple((pltpu.VMEM(shape, F32) for shape...]
    unnamed x4 -> x2, local copies, waits for them, and re-layouts: 3.99 us -> 0.01 us
where the time goes in v3:
time: 88.6 us; the launch traced here: 88.4 us
  Pallas kernels  87.8 us (99%)
    pallas_call x1, Pallas kernels, body(): pl.pallas_call(kernel, out_shape=tuple((pltpu.VMEM(shape, F32) for shape...  85.7 us
    pallas_call x1, Pallas kernels, body(): pl.pallas_call(finish, out_shape=(jax.ShapeDtypeStruct((2, 16, 32, 512),...  2.11 us

profile of v3, /device:TPU:1, one launch (start us, length us, event | category | flops | bytes accessed | tf_op | source)
XLA Modules:
  0.0 88.4 jit_solution(4212145273212082040)
XLA Ops:
  0.6 0.0 copy-start
  0.6 85.7 %step.1 = (f32[2,16,48,512]{3,2,1,0:T(8,128)S(1)}, f32[2,16,32,512]{3,2,1,0:T(8,128)S(1)}, f32[16,32,512]{2,1,0:T(8,128)S(1)}, f32[2,3,32,512]{3,2,1,0:T(8,128)S...) custom-call(f32[2,16,32,512]{3,2,1,0:T(8,128)} %order_hbm.1, ...), custom_call_target="tpu_custom_call" | custom-call | tf_op jit(solution)/shard_map/step/pallas_call | solution.py:713
  86.3 0.0 copy-done
  86.3 2.1 %finish.1 = (f32[2,16,32,512]{3,2,1,0:T(8,128)}, f32[2,3,32,512]{3,2,1,0:T(8,128)}) custom-call(f32[2,16,48,512]{3,2,1,0:T(8,128)S(1)} %get-tuple-element.9.middle, f32[2,16,32,512]{3,2,1,0:T(8,128)S(1)} %get-tuple-element.10.base, f32[16,32,512]{2,1,0:T(8,128)S(1)} %get-tuple-element.11.outer_in2, f32[2,3,32,512]{3,2,1,0:T(8,128)S(1)} %get-tuple-element.12.final, ...), custom_call_target="tpu_custom_call" | custom-call | tf_op jit(solution)/shard_map/finish/pallas_call | solution.py:756
Async XLA Ops:
  0.6 85.7 %copy-start = (f32[16,3]{0,1:T(4,128)S(1)}, f32[16,3]{0,1:T(4,128)}, u32[]{:S(2)}) copy-start(f32[16,3]{0,1:T(4,128)} %param.23) | copy-start | bytes 580

commit v4 on v3

--- a/solution.py
+++ b/solution.py
@@ -292,8 +292,9 @@
         )
         return carry
 
+    meet(1)
     lax.fori_loop(0, 32, green_step, 0)
-    meet(1)
+    meet(2)
 
     def to_columns(target, half, slots):
         for j in range(4):
@@ -311,7 +312,7 @@
 
     for copy in halo:
         copy.wait_recv()
-    meet(2)
+    meet(3)
     unpack(first, row_in)
     for layer in range(2):
         mob[layer, 40:41, :] = row_in[0, 32 + layer]
@@ -361,7 +362,7 @@
         base[layer, i, 8 * s : 8 * s + 8, :] = value
 
     update(first, col_in, inner, to_middle)
-    meet(3)
+    meet(4)
     for s in range(4):
         totals = [jnp.zeros((8, 512), F32)] * 3
         for i in range(16):
@@ -371,47 +372,17 @@
         for k in range(3):
             eig[inner, k, 8 * s : 8 * s + 8, :] = totals[k]
             eig[outer, k, 8 * s : 8 * s + 8, :] = jnp.zeros((8, 512), F32)
+    eig_copy = remote(eig.at[other], eig_in.at[c], core_send.at[1], core_recv.at[1], core_peer)
+
+    @pl.when(c == 1)
+    def _():
+        eig_copy.start()
+
+    meet(5)
     update(first, col_in, outer, to_middle)
-    meet(4)
 
     lame_copy.wait_recv()
     stiff_columns(1 - c, lame_in[1 - c, 0], lame_in[1 - c, 1])
-
-    for k in range(CHUNKS):
-        outer_copy(k).wait_recv()
-        if k == 2:
-            meet(5)
-
-        def add(s, carry):
-            at, at2 = pl.ds(pl.multiple_of(8 + 8 * s, 8), 8), pl.ds(pl.multiple_of(8 * s, 8), 8)
-            m05 = 0.05 * mob[outer, at, :]
-            totals = [eig[outer, n, at2, :] for n in range(3)]
-            for i in range(CHUNK):
-                j = k * CHUNK + i
-                v = middle[outer, j, at, :] + m05 * outer_in[j, at2, :]
-                middle[outer, j, at, :] = v
-                v = v * v
-                totals = [totals[n] + v * eigen_s[n, j] for n in range(3)]
-            for n in range(3):
-                eig[outer, n, at2, :] = totals[n]
-            return carry
-
-        lax.fori_loop(0, 4, add, 0)
-        if k < EARLY:
-            outer_copy2(k).start()
-
-    eig_copy = remote(eig.at[other], eig_in.at[c], core_send.at[1], core_recv.at[1], core_peer)
-    eig_copy.start()
-    to_columns(eig_t, c, (eig[mine, 0], eig[mine, 2], eig[mine, 1], eig[mine, 2]))
-    halo2 = [
-        remote(row_out2.at[0], row_in2.at[0], halo_send.at[3], halo_recv.at[3], row_up),
-        remote(row_out2.at[1], row_in2.at[1], halo_send.at[4], halo_recv.at[4], row_down),
-        remote(col_out2, col_in2, halo_send.at[5], halo_recv.at[5], core_peer),
-    ]
-
-    eig_copy.wait_recv()
-    far = [eig_in[1 - c, k] for k in range(3)]
-    to_columns(eig_t, 1 - c, (far[0], far[2], far[1], far[2]))
 
     lane1 = lax.broadcasted_iota(jnp.int32, (128, 128), 1)
     start = jnp.where(
@@ -419,8 +390,6 @@
     )
     for n1 in range(8):
         strain[n1] = start
-    for load in loads[3:]:
-        load.wait()
 
     even16 = (lane16 // 32) % 2 == 0
     lane_all = lax.broadcasted_iota(jnp.int32, (128, 128), 1)
@@ -439,7 +408,7 @@
         x, y, z = (pltpu.roll(p[k], 32 + 32 * k, 1) for k in range(3))
         return list(p) + [jnp.where(slot == 0, x, jnp.where(slot == 1, y, z))]
 
-    def sweep(it, carry):
+    def columns_forward(it):
         def stage(t, carry):
             rows = pl.ds(pl.multiple_of(t * 16, 16), 16)
             x = []
@@ -489,6 +458,56 @@
 
         lax.fori_loop(0, 4, forward, 0)
         pltpu.make_async_copy(send1.at[it, r], recv1.at[it, r], all_recv.at[2 * it]).start()
+
+    def columns_start():
+        for load in loads[3:]:
+            load.wait()
+        eig_copy.wait_recv()
+        for half, values in ((c, eig.at[mine]), (1 - c, eig_in.at[1 - c])):
+            fields = [values[k] for k in range(3)]
+            to_columns(eig_t, half, (fields[0], fields[2], fields[1], fields[2]))
+        columns_forward(0)
+
+    @pl.when(c == 0)
+    def _():
+        columns_start()
+
+    for k in range(CHUNKS):
+        outer_copy(k).wait_recv()
+
+        def add(s, carry):
+            at, at2 = pl.ds(pl.multiple_of(8 + 8 * s, 8), 8), pl.ds(pl.multiple_of(8 * s, 8), 8)
+            m05 = 0.05 * mob[outer, at, :]
+            totals = [eig[outer, n, at2, :] for n in range(3)]
+            for i in range(CHUNK):
+                j = k * CHUNK + i
+                v = middle[outer, j, at, :] + m05 * outer_in[j, at2, :]
+                middle[outer, j, at, :] = v
+                v = v * v
+                totals = [totals[n] + v * eigen_s[n, j] for n in range(3)]
+            for n in range(3):
+                eig[outer, n, at2, :] = totals[n]
+            return carry
+
+        lax.fori_loop(0, 4, add, 0)
+        if k < EARLY:
+            outer_copy2(k).start()
+
+    halo2 = [
+        remote(row_out2.at[0], row_in2.at[0], halo_send.at[3], halo_recv.at[3], row_up),
+        remote(row_out2.at[1], row_in2.at[1], halo_send.at[4], halo_recv.at[4], row_down),
+        remote(col_out2, col_in2, halo_send.at[5], halo_recv.at[5], core_peer),
+    ]
+
+    @pl.when(c == 0)
+    def _():
+        eig_copy.start()
+
+    @pl.when(c == 1)
+    def _():
+        columns_start()
+
+    def sweep(it, carry):
         outer_copy2(2 * it + 1).start()
 
         @pl.when(it == 0)
@@ -518,8 +537,8 @@
                     at = (slice(16 * k1, 16 * k1 + 16), slice(128 * half, 128 * half + 128))
                     lxh[at], lxl[at] = parts(z[half])
 
-        def middle_stage(q, carry):
-            rows = pl.ds(pl.multiple_of(q * 128, 128), 128)
+        for q in range(4):
+            rows = slice(q * 128, q * 128 + 128)
             spectrum = dot3(lxh[rows, :], lxl[rows, :], bfh[...], bfl[...])
             group = pl.ds(8 * q, 8)
             g0 = green[0, group].reshape(128, 128)
@@ -539,9 +558,6 @@
                 real, imag = back[16 * j : 16 * j + 16, 0:128], back[16 * j : 16 * j + 16, 128:256]
                 flat[k1, 0] = real * cosine - imag * sine
                 flat[k1, 1] = imag * cosine + real * sine
-            return carry
-
-        lax.fori_loop(0, 4, middle_stage, 0)
 
         for ka in range(4):
             y = eight([(flat[ka + 4 * kb, 0], flat[ka + 4 * kb, 1]) for kb in range(8)], 1)
@@ -584,7 +600,7 @@
         update(middle, col_in2, it, to_base)
         pltpu.make_async_copy(recv2.at[it], recv2.at[it], all_recv.at[2 * it + 1]).wait()
 
-        def inverse(kind, carry):
+        for kind in range(4):
             group = pl.ds(8 * kind, 8)
             v = unpack3([recv2[it, group, n].reshape(64, 128) for n in range(3)])
             for half in range(2):
@@ -595,9 +611,6 @@
             result = product(tih, til, kind)
             flat[pl.ds(8 * kind, 8), 0] = result[0:128].reshape(8, 16, 128)
             flat[pl.ds(8 * kind, 8), 1] = result[128:256].reshape(8, 16, 128)
-            return carry
-
-        lax.fori_loop(0, 4, inverse, 0)
 
         def unstage(t, carry):
             rows = pl.ds(pl.multiple_of(t * 16, 16), 16)
@@ -623,6 +636,11 @@
             return carry
 
         lax.fori_loop(0, 8, unstage, 0)
+
+        @pl.when(it < ITERS - 1)
+        def _():
+            columns_forward(it + 1)
+
         return carry
 
     lax.fori_loop(0, ITERS, sweep, 0)

time: 88.6 us -> 83.8 us (0.946)
  Pallas kernels: 87.8 us -> 83 us
    pallas_call x1, Pallas kernels: 85.7 us -> 80.9 us  [body(): pl.pallas_call(kernel, out_shape=tuple((pltpu.VMEM(shape, F32) for shape...]
where the time goes in v4:
time: 83.8 us; the launch traced here: 83.6 us
  Pallas kernels  83 us (99%)
    pallas_call x1, Pallas kernels, body(): pl.pallas_call(kernel, out_shape=tuple((pltpu.VMEM(shape, F32) for shape...  80.9 us
    pallas_call x1, Pallas kernels, body(): pl.pallas_call(finish, out_shape=(jax.ShapeDtypeStruct((2, 16, 32, 512),...  2.11 us

profile of v4, /device:TPU:1, one launch (start us, length us, event | category | flops | bytes accessed | tf_op | source)
XLA Modules:
  0.0 83.6 jit_solution(12537798902910556907)
XLA Ops:
  0.6 0.0 copy-start
  0.6 80.9 %step.1 = (f32[2,16,48,512]{3,2,1,0:T(8,128)S(1)}, f32[2,16,32,512]{3,2,1,0:T(8,128)S(1)}, f32[16,32,512]{2,1,0:T(8,128)S(1)}, f32[2,3,32,512]{3,2,1,0:T(8,128)S...) custom-call(f32[2,16,32,512]{3,2,1,0:T(8,128)} %order_hbm.1, ...), custom_call_target="tpu_custom_call" | custom-call | tf_op jit(solution)/shard_map/step/pallas_call | solution.py:731
  81.5 0.0 copy-done
  81.5 2.1 %finish.1 = (f32[2,16,32,512]{3,2,1,0:T(8,128)}, f32[2,3,32,512]{3,2,1,0:T(8,128)}) custom-call(f32[2,16,48,512]{3,2,1,0:T(8,128)S(1)} %get-tuple-element.9.middle, f32[2,16,32,512]{3,2,1,0:T(8,128)S(1)} %get-tuple-element.10.base, f32[16,32,512]{2,1,0:T(8,128)S(1)} %get-tuple-element.11.outer_in2, f32[2,3,32,512]{3,2,1,0:T(8,128)S(1)} %get-tuple-element.12.final, ...), custom_call_target="tpu_custom_call" | custom-call | tf_op jit(solution)/shard_map/finish/pallas_call | solution.py:774
Async XLA Ops:
  0.6 80.9 %copy-start = (f32[16,3]{0,1:T(4,128)S(1)}, f32[16,3]{0,1:T(4,128)}, u32[]{:S(2)}) copy-start(f32[16,3]{0,1:T(4,128)} %param.23) | copy-start | bytes 580

commit v5 on v4

--- a/solution.py
+++ b/solution.py
@@ -462,8 +462,9 @@
     def columns_start():
         for load in loads[3:]:
             load.wait()
-        eig_copy.wait_recv()
         for half, values in ((c, eig.at[mine]), (1 - c, eig_in.at[1 - c])):
+            if half is not c:
+                eig_copy.wait_recv()
             fields = [values[k] for k in range(3)]
             to_columns(eig_t, half, (fields[0], fields[2], fields[1], fields[2]))
         columns_forward(0)
@@ -508,7 +509,11 @@
         columns_start()
 
     def sweep(it, carry):
-        outer_copy2(2 * it + 1).start()
+
+        @pl.when(it == 1)
+        def _():
+            outer_copy2(2).start()
+
 
         @pl.when(it == 0)
         def _():
@@ -592,11 +597,11 @@
 
         @pl.when(it == 0)
         def _():
-            outer_copy2(2).start()
             for copy in halo2:
                 copy.wait_recv()
             unpack(middle, row_in2)
 
+        outer_copy2(2 * it + 1).start()
         update(middle, col_in2, it, to_base)
         pltpu.make_async_copy(recv2.at[it], recv2.at[it], all_recv.at[2 * it + 1]).wait()
 
@@ -645,22 +650,30 @@
 
     lax.fori_loop(0, ITERS, sweep, 0)
 
-    def to_rows(half, layer, target):
-        for j in range(4):
-            block = strain[4 * half + j].T
-            lanes = slice(128 * j, 128 * j + 128)
-            target[layer, 0, :, lanes] = block[0:32]
-            target[layer, 1, :, lanes] = block[64:96]
-            target[layer, 2, :, lanes] = block[32:64]
-
-    to_rows(1 - c, 0, eig_in)
-    final_copy = remote(eig_in.at[0], final.at[mine], core_send.at[2], core_recv.at[2], core_peer)
-    final_copy.start()
-    to_rows(c, mine, final)
-    remote(eig_in.at[0], final.at[other], core_send.at[2], core_recv.at[2], core_peer).wait_recv()
+    def to_rows(half, layer, target, j):
+        block = strain[4 * half + j].T
+        lanes = slice(128 * j, 128 * j + 128)
+        target[layer, 0, :, lanes] = block[0:32]
+        target[layer, 1, :, lanes] = block[64:96]
+        target[layer, 2, :, lanes] = block[32:64]
+
+    def final_copy(layer, j):
+        lanes = pl.ds(128 * j, 128)
+        return remote(
+            eig_in.at[0, :, :, lanes], final.at[layer, :, :, lanes],
+            core_send.at[2 + j], core_recv.at[2 + j], core_peer,
+        )
+
+    for j in range(4):
+        to_rows(1 - c, 0, eig_in, j)
+        final_copy(mine, j).start()
+    for j in range(4):
+        to_rows(c, mine, final, j)
+    for j in range(4):
+        final_copy(other, j).wait_recv()
     for k in range(CHUNKS):
         outer_copy2(k).wait_recv()
-    for copy in halo + halo2 + [lame_copy, eig_copy, final_copy]:
+    for copy in halo + halo2 + [lame_copy, eig_copy] + [final_copy(mine, j) for j in range(4)]:
         copy.wait_send()
     for k in range(CHUNKS):
         outer_copy(k).wait_send()
@@ -763,7 +776,7 @@
         + [pltpu.VMEM((512, 256), BF16)] * 2
         + [
             pltpu.SemaphoreType.DMA((n,))
-            for n in (12, 6, 6, 2 * CHUNKS, 2 * CHUNKS, 3, 3, 2 * ITERS, 2 * ITERS)
+            for n in (12, 6, 6, 2 * CHUNKS, 2 * CHUNKS, 6, 6, 2 * ITERS, 2 * ITERS)
         ]
         + [pltpu.SemaphoreType.REGULAR((5,))],
         compiler_params=pltpu.CompilerParams(

time: 83.8 us -> 83.5 us (level)
  no operation moved by 1% of the time
where the time goes in v5:
time: 83.5 us; the launch traced here: 83.3 us
  Pallas kernels  82.7 us (99%)
    pallas_call x1, Pallas kernels, body(): pl.pallas_call(kernel, out_shape=tuple((pltpu.VMEM(shape, F32) for shape...  80.6 us
    pallas_call x1, Pallas kernels, body(): pl.pallas_call(finish, out_shape=(jax.ShapeDtypeStruct((2, 16, 32, 512),...  2.11 us

profile of v5, /device:TPU:1, one launch (start us, length us, event | category | flops | bytes accessed | tf_op | source)
XLA Modules:
  0.0 83.3 jit_solution(8647324682992910113)
XLA Ops:
  0.6 0.0 copy-start
  0.6 80.6 %step.1 = (f32[2,16,48,512]{3,2,1,0:T(8,128)S(1)}, f32[2,16,32,512]{3,2,1,0:T(8,128)S(1)}, f32[16,32,512]{2,1,0:T(8,128)S(1)}, f32[2,3,32,512]{3,2,1,0:T(8,128)S...) custom-call(f32[2,16,32,512]{3,2,1,0:T(8,128)} %order_hbm.1, ...), custom_call_target="tpu_custom_call" | custom-call | tf_op jit(solution)/shard_map/step/pallas_call | solution.py:744
  81.2 0.0 copy-done
  81.2 2.1 %finish.1 = (f32[2,16,32,512]{3,2,1,0:T(8,128)}, f32[2,3,32,512]{3,2,1,0:T(8,128)}) custom-call(f32[2,16,48,512]{3,2,1,0:T(8,128)S(1)} %get-tuple-element.9.middle, f32[2,16,32,512]{3,2,1,0:T(8,128)S(1)} %get-tuple-element.10.base, f32[16,32,512]{2,1,0:T(8,128)S(1)} %get-tuple-element.11.outer_in2, f32[2,3,32,512]{3,2,1,0:T(8,128)S(1)} %get-tuple-element.12.final, ...), custom_call_target="tpu_custom_call" | custom-call | tf_op jit(solution)/shard_map/finish/pallas_call | solution.py:787
Async XLA Ops:
  0.6 80.6 %copy-start = (f32[16,3]{0,1:T(4,128)S(1)}, f32[16,3]{0,1:T(4,128)}, u32[]{:S(2)}) copy-start(f32[16,3]{0,1:T(4,128)} %param.23) | copy-start | bytes 580

commit v6 on v4

--- a/solution.py
+++ b/solution.py
@@ -19,7 +19,7 @@
 CHUNK = 4
 CHUNKS = 16 // CHUNK
 UNROLL = 4
-EARLY = 1
+EARLY = 0
 
 
 def split_table(values):
@@ -462,8 +462,9 @@
     def columns_start():
         for load in loads[3:]:
             load.wait()
-        eig_copy.wait_recv()
         for half, values in ((c, eig.at[mine]), (1 - c, eig_in.at[1 - c])):
+            if half is not c:
+                eig_copy.wait_recv()
             fields = [values[k] for k in range(3)]
             to_columns(eig_t, half, (fields[0], fields[2], fields[1], fields[2]))
         columns_forward(0)
@@ -508,7 +509,7 @@
         columns_start()
 
     def sweep(it, carry):
-        outer_copy2(2 * it + 1).start()
+        outer_copy2(2 * it).start()
 
         @pl.when(it == 0)
         def _():
@@ -592,11 +593,11 @@
 
         @pl.when(it == 0)
         def _():
-            outer_copy2(2).start()
             for copy in halo2:
                 copy.wait_recv()
             unpack(middle, row_in2)
 
+        outer_copy2(2 * it + 1).start()
         update(middle, col_in2, it, to_base)
         pltpu.make_async_copy(recv2.at[it], recv2.at[it], all_recv.at[2 * it + 1]).wait()
 

time: 83.8 us -> 83.7 us (level)
  no operation moved by 1% of the time
where the time goes in v6:
time: 83.7 us; the launch traced here: 83.5 us
  Pallas kernels  82.9 us (99%)
    pallas_call x1, Pallas kernels, body(): pl.pallas_call(kernel, out_shape=tuple((pltpu.VMEM(shape, F32) for shape...  80.8 us
    pallas_call x1, Pallas kernels, body(): pl.pallas_call(finish, out_shape=(jax.ShapeDtypeStruct((2, 16, 32, 512),...  2.11 us

profile of v6, /device:TPU:1, one launch (start us, length us, event | category | flops | bytes accessed | tf_op | source)
XLA Modules:
  0.0 83.5 jit_solution(2736541214892915425)
XLA Ops:
  0.6 0.0 copy-start
  0.6 80.8 %step.1 = (f32[2,16,48,512]{3,2,1,0:T(8,128)S(1)}, f32[2,16,32,512]{3,2,1,0:T(8,128)S(1)}, f32[16,32,512]{2,1,0:T(8,128)S(1)}, f32[2,3,32,512]{3,2,1,0:T(8,128)S...) custom-call(f32[2,16,32,512]{3,2,1,0:T(8,128)} %order_hbm.1, ...), custom_call_target="tpu_custom_call" | custom-call | tf_op jit(solution)/shard_map/step/pallas_call | solution.py:732
  81.4 0.0 copy-done
  81.4 2.1 %finish.1 = (f32[2,16,32,512]{3,2,1,0:T(8,128)}, f32[2,3,32,512]{3,2,1,0:T(8,128)}) custom-call(f32[2,16,48,512]{3,2,1,0:T(8,128)S(1)} %get-tuple-element.9.middle, f32[2,16,32,512]{3,2,1,0:T(8,128)S(1)} %get-tuple-element.10.base, f32[16,32,512]{2,1,0:T(8,128)S(1)} %get-tuple-element.11.outer_in2, f32[2,3,32,512]{3,2,1,0:T(8,128)S(1)} %get-tuple-element.12.final, ...), custom_call_target="tpu_custom_call" | custom-call | tf_op jit(solution)/shard_map/finish/pallas_call | solution.py:775
Async XLA Ops:
  0.6 80.8 %copy-start = (f32[16,3]{0,1:T(4,128)S(1)}, f32[16,3]{0,1:T(4,128)}, u32[]{:S(2)}) copy-start(f32[16,3]{0,1:T(4,128)} %param.23) | copy-start | bytes 580
